TPU v7x, 512 devices: a whole 4x4x16 slice. The times are simulated.
512 devices in a mesh: row: 8 (over z_lo), col: 4 (over x), blk: 16 (over z_hi, y, core).
Axes of the slice: x: 4, y: 4, z: 16 (z_hi: 2, z_lo: 8; z = z_hi * 8 + z_lo), core: 2. Of those that a mesh axis runs over, the one named last changes fastest.
Arguments:
- theta: float32 [64, 256, 1024], P('blk', 'row', 'col'), may hold values from -6 to 6
- section: float32 [64, 256, 1024], P('blk', 'row', 'col'), may hold values from -6 to 6
- velocity: float32 [3, 32, 128, 512], P(None, None, ('row', 'blk'), 'col'), may hold values from -6 to 6
- lower_plane: int32 [64], replicated, may hold values from 0 to 30, as said below
- weight_x: float32 [64], P('blk'), may hold values from 0 to 1
- metric_x: float32 [64], P('blk'), may hold values from 0.5 to 2
- first_x: float32 [4, 4], replicated
- first_y: float32 [32, 32], replicated
- first_z: float32 [256, 256], replicated
- second_x: float32 [4, 4], replicated
- second_y: float32 [32, 32], replicated
- second_z: float32 [256, 256], replicated
Outputs:
- theta_new: float32 [64, 256, 1024], P('blk', 'row', 'col')
- section_new: float32 [64, 256, 1024], P('blk', 'row', 'col')
Inputs may be any that keep to these rules, and one draw needn't show every extreme that they name: lower_plane[i] differs from i // 2 by at most one; in every aligned block of 4 fine planes the planes lower_plane[i] and lower_plane[i] + 1 lie within 5 consecutive coarse planes, and some block needs all 5.
All inputs are finite; a program needn't handle non-finite values.
Results may differ from a plain program's by a relative error of at most 0.00005.
Values sent between devices are 32-bit elements; how exact they have to be, the bound alone decides.
A program may use at most 64 MiB of HBM per device.

v0:
```python
import jax
import jax.numpy as jnp
from jax import lax
from jax.sharding import PartitionSpec as P

HIGHEST_PRECISION = lax.Precision.HIGHEST
TIME_STEP = 0.2
DIFFUSIVITY = 0.2
MEAN_GRADIENT = 1.0
SECTION_DECAY = -5.0 / 9.0
SECTION_WEIGHT = 15.0 / 16.0


def padded_2(cells, sides, width):
    for axis, dim in sides:
        count = lax.axis_size(axis)
        head = lax.slice_in_dim(cells, 0, width, axis=dim)
        tail = lax.slice_in_dim(cells, cells.shape[dim] - width, cells.shape[dim], axis=dim)
        cells = jnp.concatenate(
            [
                lax.ppermute(tail, axis, [(i, (i + 1) % count) for i in range(count)]),
                cells,
                lax.ppermute(head, axis, [((i + 1) % count, i) for i in range(count)]),
            ],
            axis=dim,
        )
    return cells


def stencil_first(padded, axis_index):
    length = padded.shape[axis_index] - 4

    def offset_slice(offset):
        return lax.slice_in_dim(padded, 2 + offset, 2 + offset + length, axis=axis_index)

    return 7.0 / 9.0 * (offset_slice(1) - offset_slice(-1)) + 1.0 / 36.0 * (
        offset_slice(2) - offset_slice(-2)
    )


def stencil_second(padded, axis_index):
    length = padded.shape[axis_index] - 4

    def offset_slice(offset):
        return lax.slice_in_dim(padded, 2 + offset, 2 + offset + length, axis=axis_index)

    middle = offset_slice(0)
    return 12.0 / 11.0 * (offset_slice(1) - 2.0 * middle + offset_slice(-1)) + 3.0 / 44.0 * (
        offset_slice(2) - 2.0 * middle + offset_slice(-2)
    )


def along_axis(matrix, values, axis_index):
    patterns = {1: "ij,ajyz->aiyz", 2: "ij,axjz->axiz", 3: "ij,axyj->axyi"}
    return jnp.einsum(patterns[axis_index], matrix, values, precision=HIGHEST_PRECISION)


def refine_rows(padded):
    middle = padded[:, :, 1:-1]
    lower_rows = padded[:, :, :-2]
    upper_rows = padded[:, :, 2:]
    even_rows = 0.75 * middle + 0.25 * lower_rows
    odd_rows = 0.75 * middle + 0.25 * upper_rows
    stacked = jnp.stack((even_rows, odd_rows), axis=3)
    return stacked.reshape(middle.shape[0], middle.shape[1], 2 * middle.shape[2], middle.shape[3])


def refine_columns(values_in):
    middle = values_in[..., 1:-1]
    left_cells = values_in[..., :-2]
    right_cells = values_in[..., 2:]
    even_cells = 0.75 * middle + 0.25 * left_cells
    odd_cells = 0.75 * middle + 0.25 * right_cells
    stacked = jnp.stack((even_cells, odd_cells), axis=-1)
    return stacked.reshape(middle.shape[0], middle.shape[1], middle.shape[2], 2 * middle.shape[3])


def direction(pair, first_matrix, second_matrix, axis_index):
    slopes = along_axis(first_matrix, stencil_first(pair, axis_index), axis_index)
    curvature = along_axis(second_matrix, stencil_second(pair[0:1], axis_index), axis_index)[0]
    return (slopes[0], slopes[1], curvature)


def local(
    theta,
    section,
    velocity,
    lower_plane,
    weight_x,
    metric_x,
    first_x,
    first_y,
    first_z,
    second_x,
    second_y,
    second_z,
):
    blocks = lax.axis_size("blk")
    own_index = lax.axis_index("blk")
    planes_here = theta.shape[0]
    slot_count = planes_here // 2 + 3
    coarse_planes = velocity.shape[1]
    grouped = lower_plane.reshape(blocks, planes_here)
    firsts = jnp.min(grouped, axis=1)
    slot_range = jnp.arange(slot_count, dtype=jnp.int32)
    wanted = jnp.clip(firsts[:, None] + slot_range[None, :], 0, coarse_planes - 1)
    own_lower = lax.dynamic_slice_in_dim(lower_plane, own_index * planes_here, planes_here)
    slot_of = own_lower - jnp.min(own_lower)
    fraction = weight_x[:, None]
    mixing = (1.0 - fraction) * (slot_of[:, None] == slot_range[None, :]).astype(
        jnp.float32
    ) + fraction * (slot_of[:, None] + 1 == slot_range[None, :]).astype(jnp.float32)
    picked = velocity[:, wanted]
    arrived = lax.all_to_all(picked, "blk", split_axis=1, concat_axis=3, tiled=True)[:, 0]
    local_planes = jnp.einsum("is,asyz->aiyz", mixing, arrived, precision=HIGHEST_PRECISION)
    rimmed = padded_2(local_planes, (("row", 2), ("col", 3)), 1)
    flow_fine = refine_columns(refine_rows(rimmed))
    flux_x = flow_fine[0] * theta
    flux_y = flow_fine[1] * theta
    flux_z = flow_fine[2] * theta
    stretch = metric_x[:, None, None]
    padded = padded_2(
        jnp.stack((theta, flux_x, flux_y, flux_z)), (("blk", 1), ("row", 2), ("col", 3)), 2
    )
    pair_x = padded[0:2, :, 2:-2, 2:-2]
    pair_y = jnp.stack((padded[0], padded[2]))[:, 2:-2, :, 2:-2]
    pair_z = jnp.stack((padded[0], padded[3]))[:, 2:-2, 2:-2, :]
    slope_x, flux_slope_x, bend_x = direction(pair_x, first_x, second_x, 1)
    slope_y, flux_slope_y, bend_y = direction(pair_y, first_y, second_y, 2)
    slope_z, flux_slope_z, bend_z = direction(pair_z, first_z, second_z, 3)
    slope_x = stretch * slope_x
    divergence = stretch * flux_slope_x + flux_slope_y + flux_slope_z
    advect = 0.5 * (
        flow_fine[0] * slope_x + flow_fine[1] * slope_y + flow_fine[2] * slope_z + divergence
    )
    laplace = stretch * stretch * bend_x + bend_y + bend_z
    tendency = -advect - MEAN_GRADIENT * flow_fine[1] + DIFFUSIVITY * laplace
    section_new = SECTION_DECAY * section + TIME_STEP * tendency
    theta_new = theta + SECTION_WEIGHT * section_new
    return (theta_new, section_new)


def solution(mesh):
    placed = (
        P("blk", "row", "col"),
        P("blk", "row", "col"),
        P(None, None, ("row", "blk"), "col"),
        P(),
        P("blk"),
        P("blk"),
        P(),
        P(),
        P(),
        P(),
        P(),
        P(),
    )
    return jax.shard_map(
        local,
        mesh=mesh,
        in_specs=placed,
        out_specs=(P("blk", "row", "col"), P("blk", "row", "col")),
        check_vma=False,
    )
```

profile of v0, /device:TPU:25, one launch (start us, length us, event | category | flops | bytes accessed | tf_op | source)
XLA Modules:
  0.0 148.7 jit_solution(1286701751989444346)
XLA Ops:
  4.1 18.3 %all-to-all-start = ((f32[3,16,5,1,128]{4,3,2,0,1:T(1,128)}), f32[3,16,5,1,128]{4,3,2,0,1:T(1,128)S(1)}, u32[]{:S(2)}, u32[]{:S(2)}) async-start(f32[3,16,5,1,128]{4,3,2,0,1:T(1,128)} %copy.236), calls=%async_computation | async-start | bytes 245760 | tf_op jit(solution)/shard_map/all_to_all | solution.py:114
  22.4 1.4 dynamic-slice_reduce_fusion
  23.7 1.4 broadcast_add_fusion
  25.8 10.0 %all-to-all-done = f32[3,16,5,1,128]{4,3,2,0,1:T(1,128)S(1)} async-done(((f32[3,16,5,1,128]{4,3,2,0,1:T(1,128)}), f32[3,16,5,1,128]{4,3,2,0,1:T(1,128)S(1)}, u32[]{:S(2)}, u32[]{:S(2)}) %all-to-all-start) | async-done | bytes 122912 | tf_op jit(solution)/shard_map/all_to_all | solution.py:114
  36.8 6.5 %collective-permute-start = (f32[3,4,1,128]{3,1,2,0:T(4,128)S(1)}, f32[3,4,1,128]{3,1,2,0:T(4,128)S(1)}, u32[]{:S(2)}, u32[]{:S(2)}) collective-permute-start(f32[3,4,1,128]{3,1,2,0:T(4,128)S(1)} %get-tuple-element.50), channel_id=1, source_target_pairs={{0,64},{64,128},{128,192},{192,256},{256,320},{320,384},{384,448},... | collective-permute-start | bytes 18440 | tf_op jit(solution)/shard_map/ppermute | solution.py:21
  43.3 5.4 %collective-permute-start.1 = (f32[3,4,1,128]{3,1,2,0:T(4,128)S(1)}, f32[3,4,1,128]{3,1,2,0:T(4,128)S(1)}, u32[]{:S(2)}, u32[]{:S(2)}) collective-permute-start(f32[3,4,1,128]{3,1,2,0:T(4,128)S(1)} %get-tuple-element.51), channel_id=1, source_target_pairs={{64,0},{128,64},{192,128},{256,192},{320,256},{384,320},{448,384},... | collective-permute-start | bytes 18440 | tf_op jit(solution)/shard_map/ppermute | solution.py:23
  49.6 3.1 %collective-permute-start.2 = (f32[3,4,18,1]{3,1,2,0:T(4,128)S(1)}, f32[3,4,18,1]{3,1,2,0:T(4,128)S(1)}, u32[]{:S(2)}, u32[]{:S(2)}) collective-permute-start(f32[3,4,18,1]{3,1,2,0:T(4,128)S(1)} %get-tuple-element.48), channel_id=1, source_target_pairs={{0,16},{16,32},{32,48},{48,0},{1,17},{17,33},{33,49},{49,1},{2,18}... | collective-permute-start | bytes 2600 | tf_op jit(solution)/shard_map/ppermute | solution.py:21
  52.7 3.4 %collective-permute-start.3 = (f32[3,4,18,1]{3,1,2,0:T(4,128)S(1)}, f32[3,4,18,1]{3,1,2,0:T(4,128)S(1)}, u32[]{:S(2)}, u32[]{:S(2)}) collective-permute-start(f32[3,4,18,1]{3,1,2,0:T(4,128)S(1)} %get-tuple-element.49), channel_id=1, source_target_pairs={{16,0},{32,16},{48,32},{0,48},{17,1},{33,17},{49,33},{1,49},{18,2}... | collective-permute-start | bytes 2600 | tf_op jit(solution)/shard_map/ppermute | solution.py:23
  56.3 2.2 %collective-permute-done.3 = f32[3,4,18,1]{3,1,2,0:T(4,128)S(1)} collective-permute-done((f32[3,4,18,1]{3,1,2,0:T(4,128)S(1)}, f32[3,4,18,1]{3,1,2,0:T(4,128)S(1)}, u32[]{:S(2)}, u32[]{:S(2)}) %collective-permute-start.3) | collective-permute-done | bytes 896 | tf_op jit(solution)/shard_map/ppermute | solution.py:23
  61.3 1.2 copy.247
  64.0 6.3 %collective-permute-start.5 = (f32[4,2,32,256]{3,2,1,0:T(8,128)S(1)}, f32[4,2,32,256]{3,2,1,0:T(8,128)S(1)}, u32[]{:S(2)}, u32[]{:S(2)}) collective-permute-start(f32[4,2,32,256]{3,2,1,0:T(8,128)S(1)} %get-tuple-element.34), channel_id=1, source_target_pairs={{0,1},{1,2},{2,3},{3,4},{4,5},{5,6},{6,7},{7,8},{8,9},{9,10},{10,1... | collective-permute-start | bytes 786440 | tf_op jit(solution)/shard_map/ppermute | solution.py:21
  70.3 1.9 %collective-permute-start.4 = (f32[4,2,32,256]{3,2,1,0:T(8,128)S(1)}, f32[4,2,32,256]{3,2,1,0:T(8,128)S(1)}, u32[]{:S(2)}, u32[]{:S(2)}) collective-permute-start(f32[4,2,32,256]{3,2,1,0:T(8,128)S(1)} %get-tuple-element.35), channel_id=1, source_target_pairs={{1,0},{2,1},{3,2},{4,3},{5,4},{6,5},{7,6},{8,7},{9,8},{10,9},{11,1... | collective-permute-start | bytes 786440 | tf_op jit(solution)/shard_map/ppermute | solution.py:23
  74.6 14.3 %collective-permute-done.4 = f32[4,2,32,256]{3,2,1,0:T(8,128)S(1)} collective-permute-done((f32[4,2,32,256]{3,2,1,0:T(8,128)S(1)}, f32[4,2,32,256]{3,2,1,0:T(8,128)S(1)}, u32[]{:S(2)}, u32[]{:S(2)}) %collective-permute-start.4) | collective-permute-done | bytes 262176 | tf_op jit(solution)/shard_map/ppermute | solution.py:23
  89.0 18.9 %collective-permute-start.7 = (f32[4,8,2,256]{3,1,2,0:T(8,128)S(1)}, f32[4,8,2,256]{3,1,2,0:T(8,128)S(1)}, u32[]{:S(2)}, u32[]{:S(2)}) collective-permute-start(f32[4,8,2,256]{3,1,2,0:T(8,128)S(1)} %copy.292), channel_id=1, source_target_pairs={{64,0},{128,64},{192,128},{256,192},{320,256},{384,320},{448,384},... | collective-permute-start | bytes 196616 | tf_op jit(solution)/shard_map/ppermute | solution.py:23
  107.9 1.9 %collective-permute-start.6 = (f32[4,8,2,256]{3,1,2,0:T(8,128)S(1)}, f32[4,8,2,256]{3,1,2,0:T(8,128)S(1)}, u32[]{:S(2)}, u32[]{:S(2)}) collective-permute-start(f32[4,8,2,256]{3,1,2,0:T(8,128)S(1)} %copy.291), channel_id=1, source_target_pairs={{0,64},{64,128},{128,192},{192,256},{256,320},{320,384},{384,448},... | collective-permute-start | bytes 196616 | tf_op jit(solution)/shard_map/ppermute | solution.py:21
  110.1 1.4 convolution_bitcast_fusion
  112.3 7.3 %collective-permute-done.6 = f32[4,8,2,256]{3,1,2,0:T(8,128)S(1)} collective-permute-done((f32[4,8,2,256]{3,1,2,0:T(8,128)S(1)}, f32[4,8,2,256]{3,1,2,0:T(8,128)S(1)}, u32[]{:S(2)}, u32[]{:S(2)}) %collective-permute-start.6) | collective-permute-done | bytes 65568 | tf_op jit(solution)/shard_map/ppermute | solution.py:21
  120.8 2.0 %copy.256 = f32[4,8,36,2]{2,1,3,0:T(8,128)} copy(f32[4,8,36,2]{3,2,1,0:T(8,128)} %get-tuple-element.18) | data formatting | bytes 18432 | tf_op jit(solution)/shard_map/slice | solution.py:18
  123.8 4.6 %collective-permute-start.9 = (f32[4,8,36,2]{2,1,3,0:T(8,128)}, f32[4,8,36,2]{2,1,3,0:T(8,128)S(1)}, u32[]{:S(2)}, u32[]{:S(2)}) collective-permute-start(f32[4,8,36,2]{2,1,3,0:T(8,128)} %copy.257), channel_id=1, source_target_pairs={{16,0},{32,16},{48,32},{0,48},{17,1},{33,17},{49,33},{1,49},{18,2}... | collective-permute-start | bytes 27656 | tf_op jit(solution)/shard_map/ppermute | solution.py:23
  128.4 2.1 %collective-permute-start.8 = (f32[4,8,36,2]{2,1,3,0:T(8,128)}, f32[4,8,36,2]{2,1,3,0:T(8,128)S(1)}, u32[]{:S(2)}, u32[]{:S(2)}) collective-permute-start(f32[4,8,36,2]{2,1,3,0:T(8,128)} %copy.256), channel_id=1, source_target_pairs={{0,16},{16,32},{32,48},{48,0},{1,17},{17,33},{33,49},{49,1},{2,18}... | collective-permute-start | bytes 27656 | tf_op jit(solution)/shard_map/ppermute | solution.py:21
  131.5 1.4 copy.259
  132.9 1.6 %collective-permute-done.8 = f32[4,8,36,2]{2,1,3,0:T(8,128)S(1)} collective-permute-done((f32[4,8,36,2]{2,1,3,0:T(8,128)}, f32[4,8,36,2]{2,1,3,0:T(8,128)S(1)}, u32[]{:S(2)}, u32[]{:S(2)}) %collective-permute-start.8) | collective-permute-done | bytes 9248 | tf_op jit(solution)/shard_map/ppermute | solution.py:21
  136.0 1.7 %fusion.7 = (f32[2,8,36,260]{3,1,2,0:T(8,128)S(1)}, f32[2,8,36,260]{3,1,2,0:T(8,128)S(1)}) fusion(f32[4,8,36,2]{3,1,2,0:T(8,128)} %copy.260, f32[4,8,36,256]{3,1,2,0:T(8,128)S(1)} %copy-done.2, f32[4,8,36,2]{3,1,2,0:T(8,128)S(1)} %copy.258), kind=kLoop, calls=%fused_computation.15 | loop fusion | flops 2845440 | bytes 2396160 | tf_op jit(solution)/shard_map/stack | solution.py:127
  142.2 3.5 %pad_maximum_fusion = (f32[4,8,36,258]{3,2,1,0:T(8,128)S(1)}, f32[4,8,36,258]{3,2,1,0:T(8,128)S(1)}) fusion(f32[4,8,36,2]{3,2,1,0:T(8,128)S(1)} %copy.279, f32[4,8,2,256]{3,2,1,0:T(2,128)S(1)} %copy.255, f32[4,2,32,256]{3,2,1,0:T(8,128)S(1)} %collective-permute-done.4, f32[1,4,32,256]{3,2,1,0:T(8,128)S(1)} %copy.249, f32[1,4,32,256]{3,2,1,0:T(8,128)S(1)} %copy.248, ...), kind=kLoop, calls=%fused_computation.1 | loop fusion | flops 4755456 | bytes 3575808 | tf_op jit(solution)/shard_map/concatenate | solution.py:19
  (104 shorter events, 25.9 us)
Async XLA Ops:
  0.6 138.1 %copy-start = (f32[256,256]{1,0:T(8,128)S(1)}, f32[256,256]{1,0:T(8,128)}, u32[]{:S(2)}) copy-start(f32[256,256]{1,0:T(8,128)} %param.20) | copy-start | bytes 786436
  0.6 55.5 %copy-start.1 = (f32[4,32,256]{2,1,0:T(8,128)S(1)}, f32[4,32,256]{2,1,0:T(8,128)}, u32[]{:S(2)}) copy-start(f32[4,32,256]{2,1,0:T(8,128)} %param.12) | copy-start | bytes 393220
  4.1 31.6 %all-to-all-start = ((f32[3,16,5,1,128]{4,3,2,0,1:T(1,128)}), f32[3,16,5,1,128]{4,3,2,0,1:T(1,128)S(1)}, u32[]{:S(2)}, u32[]{:S(2)}) async-start(f32[3,16,5,1,128]{4,3,2,0,1:T(1,128)} %copy.236), calls=%async_computation | async-start | bytes 245760 | tf_op jit(solution)/shard_map/all_to_all | solution.py:114
  36.8 11.9 %collective-permute-start = (f32[3,4,1,128]{3,1,2,0:T(4,128)S(1)}, f32[3,4,1,128]{3,1,2,0:T(4,128)S(1)}, u32[]{:S(2)}, u32[]{:S(2)}) collective-permute-start(f32[3,4,1,128]{3,1,2,0:T(4,128)S(1)} %get-tuple-element.50), channel_id=1, source_target_pairs={{0,64},{64,128},{128,192},{192,256},{256,320},{320,384},{384,448},... | collective-permute-start | bytes 18440 | tf_op jit(solution)/shard_map/ppermute | solution.py:21
  43.3 6.1 %collective-permute-start.1 = (f32[3,4,1,128]{3,1,2,0:T(4,128)S(1)}, f32[3,4,1,128]{3,1,2,0:T(4,128)S(1)}, u32[]{:S(2)}, u32[]{:S(2)}) collective-permute-start(f32[3,4,1,128]{3,1,2,0:T(4,128)S(1)} %get-tuple-element.51), channel_id=1, source_target_pairs={{64,0},{128,64},{192,128},{256,192},{320,256},{384,320},{448,384},... | collective-permute-start | bytes 18440 | tf_op jit(solution)/shard_map/ppermute | solution.py:23
  49.6 6.7 %collective-permute-start.2 = (f32[3,4,18,1]{3,1,2,0:T(4,128)S(1)}, f32[3,4,18,1]{3,1,2,0:T(4,128)S(1)}, u32[]{:S(2)}, u32[]{:S(2)}) collective-permute-start(f32[3,4,18,1]{3,1,2,0:T(4,128)S(1)} %get-tuple-element.48), channel_id=1, source_target_pairs={{0,16},{16,32},{32,48},{48,0},{1,17},{17,33},{33,49},{49,1},{2,18}... | collective-permute-start | bytes 2600 | tf_op jit(solution)/shard_map/ppermute | solution.py:21
  52.7 5.8 %collective-permute-start.3 = (f32[3,4,18,1]{3,1,2,0:T(4,128)S(1)}, f32[3,4,18,1]{3,1,2,0:T(4,128)S(1)}, u32[]{:S(2)}, u32[]{:S(2)}) collective-permute-start(f32[3,4,18,1]{3,1,2,0:T(4,128)S(1)} %get-tuple-element.49), channel_id=1, source_target_pairs={{16,0},{32,16},{48,32},{0,48},{17,1},{33,17},{49,33},{1,49},{18,2}... | collective-permute-start | bytes 2600 | tf_op jit(solution)/shard_map/ppermute | solution.py:23
  61.3 10.9 %copy-start.16 = (f32[4]{0:T(128)S(1)}, f32[4]{0:T(128)}, u32[]{:S(2)}) copy-start(f32[4]{0:T(128)} %param.17) | copy-start | bytes 52
  64.0 10.6 %collective-permute-start.5 = (f32[4,2,32,256]{3,2,1,0:T(8,128)S(1)}, f32[4,2,32,256]{3,2,1,0:T(8,128)S(1)}, u32[]{:S(2)}, u32[]{:S(2)}) collective-permute-start(f32[4,2,32,256]{3,2,1,0:T(8,128)S(1)} %get-tuple-element.34), channel_id=1, source_target_pairs={{0,1},{1,2},{2,3},{3,4},{4,5},{5,6},{6,7},{7,8},{8,9},{9,10},{10,1... | collective-permute-start | bytes 786440 | tf_op jit(solution)/shard_map/ppermute | solution.py:21
  70.3 18.6 %collective-permute-start.4 = (f32[4,2,32,256]{3,2,1,0:T(8,128)S(1)}, f32[4,2,32,256]{3,2,1,0:T(8,128)S(1)}, u32[]{:S(2)}, u32[]{:S(2)}) collective-permute-start(f32[4,2,32,256]{3,2,1,0:T(8,128)S(1)} %get-tuple-element.35), channel_id=1, source_target_pairs={{1,0},{2,1},{3,2},{4,3},{5,4},{6,5},{7,6},{8,7},{9,8},{10,9},{11,1... | collective-permute-start | bytes 786440 | tf_op jit(solution)/shard_map/ppermute | solution.py:23
  89.0 21.1 %copy-start.12 = (f32[4,4]{1,0:T(4,128)S(1)}, f32[4,4]{1,0:T(4,128)}, u32[]{:S(2)}) copy-start(f32[4,4]{1,0:T(4,128)} %param.18) | copy-start | bytes 196
  89.0 23.2 %collective-permute-start.7 = (f32[4,8,2,256]{3,1,2,0:T(8,128)S(1)}, f32[4,8,2,256]{3,1,2,0:T(8,128)S(1)}, u32[]{:S(2)}, u32[]{:S(2)}) collective-permute-start(f32[4,8,2,256]{3,1,2,0:T(8,128)S(1)} %copy.292), channel_id=1, source_target_pairs={{64,0},{128,64},{192,128},{256,192},{320,256},{384,320},{448,384},... | collective-permute-start | bytes 196616 | tf_op jit(solution)/shard_map/ppermute | solution.py:23
  107.9 11.6 %collective-permute-start.6 = (f32[4,8,2,256]{3,1,2,0:T(8,128)S(1)}, f32[4,8,2,256]{3,1,2,0:T(8,128)S(1)}, u32[]{:S(2)}, u32[]{:S(2)}) collective-permute-start(f32[4,8,2,256]{3,1,2,0:T(8,128)S(1)} %copy.291), channel_id=1, source_target_pairs={{0,64},{64,128},{128,192},{192,256},{256,320},{320,384},{384,448},... | collective-permute-start | bytes 196616 | tf_op jit(solution)/shard_map/ppermute | solution.py:21
  119.7 10.7 %copy-start.14 = (f32[32,32]{1,0:T(8,128)S(1)}, f32[32,32]{1,0:T(8,128)}, u32[]{:S(2)}) copy-start(f32[32,32]{1,0:T(8,128)} %param.22) | copy-start | bytes 12292
  123.8 11.0 %collective-permute-start.9 = (f32[4,8,36,2]{2,1,3,0:T(8,128)}, f32[4,8,36,2]{2,1,3,0:T(8,128)S(1)}, u32[]{:S(2)}, u32[]{:S(2)}) collective-permute-start(f32[4,8,36,2]{2,1,3,0:T(8,128)} %copy.257), channel_id=1, source_target_pairs={{16,0},{32,16},{48,32},{0,48},{17,1},{33,17},{49,33},{1,49},{18,2}... | collective-permute-start | bytes 27656 | tf_op jit(solution)/shard_map/ppermute | solution.py:23
  128.4 6.1 %collective-permute-start.8 = (f32[4,8,36,2]{2,1,3,0:T(8,128)}, f32[4,8,36,2]{2,1,3,0:T(8,128)S(1)}, u32[]{:S(2)}, u32[]{:S(2)}) collective-permute-start(f32[4,8,36,2]{2,1,3,0:T(8,128)} %copy.256), channel_id=1, source_target_pairs={{0,16},{16,32},{32,48},{48,0},{1,17},{17,33},{33,49},{49,1},{2,18}... | collective-permute-start | bytes 27656 | tf_op jit(solution)/shard_map/ppermute | solution.py:21
  142.1 4.1 %copy-start.4 = (f32[2,4,32,256]{3,1,2,0:T(4,128)S(1)}, f32[2,4,32,256]{3,1,2,0:T(4,128)}, u32[]{:S(2)}) copy-start(f32[2,4,32,256]{3,1,2,0:T(4,128)} %convolution_bitcast_fusion) | copy-start | bytes 786436
  142.1 4.1 %copy-start.5 = (f32[2,4,256,32]{2,1,3,0:T(4,128)S(1)}, f32[2,4,256,32]{2,1,3,0:T(4,128)}, u32[]{:S(2)}) copy-start(f32[2,4,256,32]{2,1,3,0:T(4,128)} %copy.370) | copy-start | bytes 786436
  142.1 4.1 %copy-start.6 = (f32[4,32,256]{2,0,1:T(4,128)S(1)}, f32[4,32,256]{2,0,1:T(4,128)}, u32[]{:S(2)}) copy-start(f32[4,32,256]{2,0,1:T(4,128)} %copy.272) | copy-start | bytes 393220
  142.1 4.1 %copy-start.7 = (f32[4,32,256]{2,0,1:T(4,128)S(1)}, f32[4,32,256]{2,0,1:T(4,128)}, u32[]{:S(2)}) copy-start(f32[4,32,256]{2,0,1:T(4,128)} %copy.266) | copy-start | bytes 393220
  142.1 4.1 %copy-start.8 = (f32[4,32,256]{2,1,0:T(8,128)S(1)}, f32[4,32,256]{2,1,0:T(8,128)}, u32[]{:S(2)}) copy-start(f32[4,32,256]{2,1,0:T(8,128)} %fusion.88) | copy-start | bytes 393220
  142.1 4.1 %copy-start.9 = (f32[1,4,32,256]{3,2,1,0:T(8,128)S(1)}, f32[1,4,32,256]{3,2,1,0:T(8,128)}, u32[]{:S(2)}) copy-start(f32[1,4,32,256]{3,2,1,0:T(8,128)} %get-tuple-element.44) | copy-start | bytes 393220
  142.2 4.1 %copy-start.10 = (f32[1,4,32,256]{3,2,1,0:T(8,128)S(1)}, f32[1,4,32,256]{3,2,1,0:T(8,128)}, u32[]{:S(2)}) copy-start(f32[1,4,32,256]{3,2,1,0:T(8,128)} %get-tuple-element.45) | copy-start | bytes 393220
  142.2 4.1 %copy-start.13 = (f32[4,32,256]{2,1,0:T(8,128)S(1)}, f32[4,32,256]{2,1,0:T(8,128)}, u32[]{:S(2)}) copy-start(f32[4,32,256]{2,1,0:T(8,128)} %param.13) | copy-start | bytes 393220
  (7 other events, 24.4 us)
where the time goes:
time: 149 us
  starting transfers between devices  72.3 us (49%)
  waiting for transfers between devices  36 us (24%)
  local copies, waits for them, and re-layouts  20.7 us (14%)
  other arithmetic  12.4 us (8%)
  matrix products  6 us (4%)
    ppermute x5, starting transfers between devices, padded_2(): lax.ppermute(head, axis, [((i + 1) % count, i) for i in range(count)])  34.1 us
    ppermute x5, starting transfers between devices, padded_2(): lax.ppermute(tail, axis, [(i, (i + 1) % count) for i in range(count)])  19.9 us
    all_to_all x1, starting transfers between devices, local(): lax.all_to_all(picked, 'blk', split_axis=1, concat_axis=3, tiled=True)[:, 0]  18.3 us
    ppermute x5, waiting for transfers between devices, padded_2(): lax.ppermute(head, axis, [((i + 1) % count, i) for i in range(count)])  17.2 us
    all_to_all x1, waiting for transfers between devices, local(): lax.all_to_all(picked, 'blk', split_axis=1, concat_axis=3, tiled=True)[:, 0]  9.97 us
    ppermute x5, waiting for transfers between devices, padded_2(): lax.ppermute(tail, axis, [(i, (i + 1) % count) for i in range(count)])  8.82 us
    dot_general x6, matrix products, along_axis(): jnp.einsum(patterns[axis_index], matrix, values, precision=HIGHEST_PRECIS...  4.98 us
    concatenate x5, other arithmetic, padded_2(): jnp.concatenate([lax.ppermute(tail, axis, [(i, (i + 1) % count) for i in...  4.13 us
  transfers between devices with their start and end apart: 11, of which 6 were waited for; matrix products, arithmetic and copies ran while one was open for 7% of the time, Pallas kernels for 0%

commit v1 on v0

v1 whole, which is shorter than its diff:
```python
import jax
import jax.numpy as jnp
from jax import lax
from jax.experimental import pallas as pl
from jax.experimental.pallas import tpu as pltpu
from jax.sharding import PartitionSpec as P

F32 = jnp.float32
BF16 = jnp.bfloat16
SLAB = 24
NN = (((1,), (0,)), ((), ()))
NT = (((1,), (1,)), ((), ()))


def split2(x):
    high = x.astype(BF16)
    return high, (x - high.astype(F32)).astype(BF16)


def split3(x):
    high = x.astype(BF16)
    rest = x - high.astype(F32)
    mid = rest.astype(BF16)
    return high, mid, (rest - mid.astype(F32)).astype(BF16)


def dot(a, b, dims=NN):
    return lax.dot_general(a, b, dims, preferred_element_type=F32)


def iota(shape, dim):
    return lax.broadcasted_iota(jnp.int32, shape, dim)


def first_weights(d):
    zero = jnp.zeros(d.shape, F32)
    return jnp.where(
        d == 1, 28.0, jnp.where(d == -1, -28.0, jnp.where(d == 2, 1.0, jnp.where(d == -2, -1.0, zero)))
    ).astype(BF16)


def second_weights(d):
    zero = jnp.zeros(d.shape, F32)
    far = jnp.abs(d)
    return jnp.where(
        far == 0, -102.0, jnp.where(far == 1, 48.0, jnp.where(far == 2, 3.0, zero))
    ).astype(BF16)


def kernel(
    lower, weight, metric, fx, sx,
    theta_in, vel_in, fy_in, sy_in, fz_in, sz_in,
    out_ref,
    theta, vel, fy, sy, fz, sz,
    xlo, xhi, wown, wlo, whi, ypack, yrecv, zpack, zrecv, vzpack, vzrecv,
    pack, buf, coef, mix, rz, m1h, m1l, m2h, m2l, my, tpad, vt, fine0, fine1, fine2, efine,
    gx, gy, gz, lap,
    in_sem, x_send, x_recv, w_send, w_recv, y_send, y_recv, z_send, z_recv, v_send, v_recv,
    a_send, a_recv, b_send, b_recv, p_send, p_recv, r_send, r_recv,
):
    row, col, blk = lax.axis_index("row"), lax.axis_index("col"), lax.axis_index("blk")
    rows, cols = lax.axis_size("row"), lax.axis_size("col")
    chip, core = blk // 2, blk % 2
    zhi, ypos = chip // 4, chip % 4

    loads = []
    for n, (src, dst) in enumerate(
        ((vel_in, vel.at[pl.ds(0, 96)]), (theta_in, theta), (fz_in, fz), (sz_in, sz), (fy_in, fy), (sy_in, sy))
    ):
        load = pltpu.make_async_copy(src, dst, in_sem.at[n])
        load.start()
        loads.append(load)

    partner = {"blk": 2 * chip + (1 - core)}
    outer = {"blk": (blk + 2 * core + 15) % 16}
    up_blk, down_blk = {"blk": (blk + 1) % 16}, {"blk": (blk + 15) % 16}
    up_row, down_row = {"row": (row + 1) % rows}, {"row": (row + rows - 1) % rows}
    up_col, down_col = {"col": (col + 1) % cols}, {"col": (col + cols - 1) % cols}
    chips, senders = [], []
    for far, dy in ((1, 0), (1, 1), (1, 2), (1, 3), (0, 1), (0, 2), (0, 3)):
        chips.append(((zhi + far) % 2) * 4 + (ypos + dy) % 4)
        senders.append(((zhi + far) % 2) * 4 + (ypos + 4 - dy) % 4)

    barrier = pltpu.get_barrier_semaphore()
    peers = [{"blk": 2 * q + core} for q in chips] + [partner, outer, up_row, down_row, up_col, down_col]
    for peer in peers:
        pl.semaphore_signal(barrier, inc=1, device_id=peer, device_id_type=pl.DeviceIdType.MESH)

    started = []

    def send(src, dst, ssem, rsem, device):
        copy = pltpu.make_async_remote_copy(
            src_ref=src, dst_ref=dst, send_sem=ssem, recv_sem=rsem,
            device_id=device, device_id_type=pl.DeviceIdType.MESH,
        )
        copy.start()
        started.append(copy)

    def arrived(dst, ssem, rsem, device):
        pltpu.make_async_remote_copy(
            src_ref=dst, dst_ref=dst, send_sem=ssem, recv_sem=rsem,
            device_id=device, device_id_type=pl.DeviceIdType.MESH,
        ).wait_recv()

    vel[pl.ds(96, 32), :] = jnp.zeros((32, 128), F32)
    loads[0].wait()
    for q in range(8):
        for base, comp, first, count in ((0, 0, 4 * q - 2, 9), (9, 1, 4 * q - 1, 7), (16, 2, 4 * q - 1, 7)):
            at = 0
            while at < count:
                plane = (first + at) % 32
                take = min(count - at, 32 - plane)
                pack[pl.ds(q * SLAB + base + at, take), :] = vel[pl.ds(comp * 32 + plane, take), :]
                at += take
    vel_t = vel[...].T
    vzpack[0] = vel_t[0:8]
    vzpack[1] = vel_t[120:128]
    loads[1].wait()
    for p in range(4):
        ypack[0, pl.ds(2 * p, 2), :] = theta[p, 0:2, :]
        ypack[1, pl.ds(2 * p, 2), :] = theta[p, 30:32, :]
    zpack[0] = theta[:, :, 0:128].reshape(128, 128).T[0:8]
    zpack[1] = theta[:, :, 128:256].reshape(128, 128).T[120:128]
    wown[...] = jnp.concatenate(
        [jnp.full((1, 128), weight[p], F32) for p in range(4)] + [jnp.zeros((4, 128), F32)], axis=0
    )

    def slot(b):
        return pl.ds(pl.multiple_of((b + 2) * SLAB, 8), SLAB)

    def part(first, offset, count):
        return pl.ds(pl.multiple_of(first + offset, 8), count)

    pl.semaphore_wait(barrier, len(peers))

    send(vzpack.at[1], vzrecv.at[0], v_send.at[0], v_recv.at[0], up_col)
    send(vzpack.at[0], vzrecv.at[1], v_send.at[1], v_recv.at[1], down_col)
    land = (blk + 2) * SLAB
    for n, q in enumerate(chips):
        send(
            pack.at[part(q * SLAB, 0, 16)], buf.at[part(land, 0, 16)],
            a_send.at[n], a_recv.at[n], {"blk": 2 * q + core},
        )
    send(theta.at[pl.ds(2, 2)], xlo, x_send.at[0], x_recv.at[0], up_blk)
    send(theta.at[pl.ds(0, 2)], xhi, x_send.at[1], x_recv.at[1], down_blk)
    send(wown, wlo, w_send.at[0], w_recv.at[0], up_blk)
    send(wown, whi, w_send.at[1], w_recv.at[1], down_blk)
    send(ypack.at[1], yrecv.at[0], y_send.at[0], y_recv.at[0], up_row)
    send(ypack.at[0], yrecv.at[1], y_send.at[1], y_recv.at[1], down_row)
    send(zpack.at[1], zrecv.at[pl.ds(0, 8)], z_send.at[0], z_recv.at[0], up_col)
    send(zpack.at[0], zrecv.at[pl.ds(8, 8)], z_send.at[1], z_recv.at[1], down_col)

    p_row, l_col = iota((128, 128), 0), iota((128, 128), 1)
    plane = p_row & 31
    comp = p_row >> 5
    place = jnp.where(comp == 0, plane & 15, jnp.where(comp == 1, 16 + (plane & 7), 24 + (plane & 7)))
    select = jnp.where((place == (l_col & 31)) & (comp < 3), 1.0, 0.0).astype(BF16)
    k_row, p_lane = iota((8, 128), 0), iota((8, 128), 1)
    plane8 = p_lane & 31
    inside0 = ((plane8 - 4 * k_row + 34) & 31) < 9
    inside1 = ((plane8 - 4 * k_row + 33) & 31) < 7
    lead = p_lane < 32
    window = (lead & inside0) | (jnp.logical_not(lead) & inside1)
    arrived(vzrecv.at[0], v_send.at[0], v_recv.at[0], down_col)
    arrived(vzrecv.at[1], v_send.at[1], v_recv.at[1], up_col)
    left, right = vzrecv[0], vzrecv[1]
    edges = jnp.concatenate(
        [
            jnp.where(window, jnp.broadcast_to(one, (8, 128)), 0.0)
            for one in (left[6:7], left[7:8], right[0:1], right[1:2])
        ],
        axis=0,
    )
    picked = sum(dot(piece, select) for piece in split3(edges))
    lane8 = iota((8, 128), 1) >> 5
    edge_rows = jnp.zeros((8, 128), F32)
    for e in range(4):
        edge_rows = jnp.where(lane8 == e, picked[8 * e : 8 * e + 8], edge_rows)
    for q in range(8):
        pack[pl.ds(q * SLAB + 23, 1), :] = edge_rows[q : q + 1]
    for n, q in enumerate(chips):
        send(
            pack.at[part(q * SLAB, 16, 8)], buf.at[part(land, 16, 8)],
            b_send.at[n], b_recv.at[n], {"blk": 2 * q + core},
        )
    own_slab = pl.ds(pl.multiple_of(chip * SLAB, 8), SLAB)
    send(pack.at[own_slab], buf.at[slot(blk)], p_send.at[7], p_recv.at[7], partner)
    buf[slot(blk), :] = pack[own_slab, :]

    for u in (2, 3, 4):
        loads[u].wait()
    loads[5].wait()
    kk, jj = iota((384, 256), 0), iota((384, 256), 1)
    at = jnp.where(kk < 256, kk, jnp.where(kk < 264, kk - 264, jnp.where(kk < 272, kk - 8, 4096)))
    stencil1, stencil2 = first_weights(at - jj), second_weights(at - jj)
    m1 = sum(dot(stencil1, piece, NT) for piece in split3(fz[...])) * (1.0 / 36.0)
    m1h[...], m1l[...] = split2(m1)
    m2 = sum(dot(stencil2, piece, NT) for piece in split3(sz[...])) * (1.0 / 44.0)
    m2h[...], m2l[...] = split2(m2)
    jy, ly = iota((32, 256), 0), iota((32, 256), 1)
    third = jnp.where(ly < 48, ly, jnp.where(ly < 96, ly - 48, jnp.where(ly < 144, ly - 96, 4096)))
    dy_ = third - 8 - jy
    my1 = sum(dot(piece, first_weights(dy_)) for piece in split3(fy[...])) * (1.0 / 36.0)
    my2 = sum(dot(piece, second_weights(dy_)) for piece in split3(sy[...])) * (1.0 / 44.0)
    both = jnp.concatenate([my1, my2], axis=0)
    high = both.astype(BF16).astype(F32)
    my[...] = jnp.where(iota((64, 256), 1) < 96, high, both - high).astype(BF16)
    kr, zr = iota((256, 384), 0), iota((256, 384), 1)
    group = (kr - 128) >> 5
    cell = jnp.where(kr < 128, kr, jnp.where(group < 2, group - 2, group + 126))
    zz = jnp.where(zr < 256, zr, jnp.where(zr < 264, zr - 264, jnp.where(zr < 272, zr - 8, 4096)))
    near = zz >> 1
    other = near + 2 * (zz & 1) - 1
    rz[...] = jnp.where(cell == near, 0.75, jnp.where(cell == other, 0.25, jnp.zeros((256, 384), F32))).astype(BF16)

    zrecv[pl.ds(16, 112), :] = jnp.zeros((112, 128), F32)
    for p in range(4):
        tpad[p, 0:8, :] = jnp.zeros((8, 256), F32)
        tpad[p, 40:48, :] = jnp.zeros((8, 256), F32)
        tpad[p, 8:40, :] = theta[p]
    arrived(zrecv.at[pl.ds(0, 8)], z_send.at[0], z_recv.at[0], down_col)
    arrived(zrecv.at[pl.ds(8, 8)], z_send.at[1], z_recv.at[1], up_col)
    side = zrecv[...].T
    th, tl = split2(theta[...].reshape(128, 256))
    sh, sl = split2(side)

    def along_z(mh, ml, ah, al, eh, el):
        h0, h1, l0, l1 = mh[0:256], mh[256:384], ml[0:256], ml[256:384]
        return dot(ah, h0) + dot(ah, l0) + dot(al, h0) + dot(eh, h1) + dot(eh, l1) + dot(el, h1)

    gz[...] = along_z(m1h[...], m1l[...], th, tl, sh, sl).reshape(4, 32, 256)
    lap[...] = along_z(m2h[...], m2l[...], th, tl, sh, sl).reshape(4, 32, 256)
    arrived(yrecv.at[0], y_send.at[0], y_recv.at[0], down_row)
    arrived(yrecv.at[1], y_send.at[1], y_recv.at[1], up_row)
    for p in range(4):
        tpad[p, 6:8, :] = yrecv[0, pl.ds(2 * p, 2), :]
        tpad[p, 40:42, :] = yrecv[1, pl.ds(2 * p, 2), :]
        ph, plow = split2(tpad[p])
        res = dot(my[:, 0:144], jnp.concatenate([ph, plow, ph], axis=0))
        gy[p] = res[0:32]
        lap[p] += res[32:64]

    for n, q in enumerate(senders):
        b = 2 * q + core
        first = (b + 2) * SLAB
        arrived(buf.at[part(first, 0, 16)], a_send.at[n], a_recv.at[n], {"blk": b})
        arrived(buf.at[part(first, 16, 8)], b_send.at[n], b_recv.at[n], {"blk": b})
        send(buf.at[slot(b)], buf.at[slot(b)], p_send.at[n], p_recv.at[n], partner)

    arrived(wlo, w_send.at[0], w_recv.at[0], down_blk)
    arrived(whi, w_send.at[1], w_recv.at[1], up_blk)
    s_row = iota((16, 128), 0)
    l_row = iota((1, 128), 1) & 31
    for t in range(8):
        low = lower[(4 * blk + t + 62) % 64]
        if t < 2:
            w = wlo[t + 2 : t + 3, :]
        elif t < 6:
            w = wown[t - 2 : t - 1, :]
        else:
            w = whi[t - 6 : t - 5, :]
        s0 = (low - 4 * chip + 34) & 31
        coef[t] = jnp.where(s_row == s0, 1.0 - w, jnp.where(s_row == s0 + 1, w, 0.0))
        for c in range(3):
            if c > 0 and not 2 <= t < 6:
                continue
            if c == 0:
                a0, a1 = low & 15, (low + 1) & 15
            else:
                a0, a1 = 8 + 8 * c + (low & 7), 8 + 8 * c + ((low + 1) & 7)
            line = 8 * c + t
            mix[pl.ds(line, 1), :] = jnp.where(l_row == a0, 1.0 - w, jnp.where(l_row == a1, w, 0.0))
    arrived(xlo, x_send.at[0], x_recv.at[0], down_blk)
    arrived(xhi, x_send.at[1], x_recv.at[1], up_blk)

    def tplane(t):
        if t < 2:
            return xlo[t]
        if t < 6:
            return theta[t - 2]
        return xhi[t - 6]

    for j in range(4):
        t = j + 2
        a, b_, c_, d_, m = tplane(t + 1), tplane(t - 1), tplane(t + 2), tplane(t - 2), tplane(t)
        one = 28.0 * (a - b_) + (c_ - d_)
        two = 48.0 * (a + b_) + 3.0 * (c_ + d_) - 102.0 * m
        for i in range(4):
            s1 = metric[i] * (fx[i, j] * (1.0 / 36.0))
            s2 = metric[i] * metric[i] * (sx[i, j] * (1.0 / 44.0))
            if j == 0:
                gx[i] = s1 * one
            else:
                gx[i] += s1 * one
            lap[i] += s2 * two

    for n, q in enumerate(senders):
        b = 2 * q + 1 - core
        arrived(buf.at[slot(b)], p_send.at[n], p_recv.at[n], partner)
    arrived(buf.at[slot(2 * chip + 1 - core)], p_send.at[7], p_recv.at[7], partner)
    send(buf.at[pl.ds(16 * SLAB, 2 * SLAB)], buf.at[pl.ds(0, 2 * SLAB)], r_send.at[0], r_recv.at[0], up_row)
    send(buf.at[pl.ds(2 * SLAB, 2 * SLAB)], buf.at[pl.ds(18 * SLAB, 2 * SLAB)], r_send.at[1], r_recv.at[1], down_row)
    buf[pl.ds(20 * SLAB, 4 * SLAB), :] = jnp.zeros((4 * SLAB, 128), F32)
    for p in range(4):
        fine1[p, 0:8, :] = jnp.zeros((8, 128), F32)
        fine1[p, 40:48, :] = jnp.zeros((8, 128), F32)
    efine[0:8, :] = jnp.zeros((8, 128), F32)
    efine[40:48, :] = jnp.zeros((8, 128), F32)
    arrived(buf.at[pl.ds(0, 2 * SLAB)], r_send.at[0], r_recv.at[0], down_row)
    arrived(buf.at[pl.ds(18 * SLAB, 2 * SLAB)], r_send.at[1], r_recv.at[1], up_row)

    def plane_of(line):
        return buf[pl.ds(line, 24, stride=SLAB), :]

    def refine_wide(value, target):
        vt[...] = value
        target[pl.ds(6, 18, stride=2), :] = 0.75 * vt[1:19] + 0.25 * vt[0:18]
        target[pl.ds(7, 18, stride=2), :] = 0.75 * vt[1:19] + 0.25 * vt[2:20]

    def refine_own(value, target):
        vt[...] = value
        target[pl.ds(0, 16, stride=2), :] = 0.75 * vt[2:18] + 0.25 * vt[1:17]
        target[pl.ds(1, 16, stride=2), :] = 0.75 * vt[2:18] + 0.25 * vt[3:19]

    refine_wide(plane_of(23), efine)
    edge_wide = efine[...]
    edge_own = efine[8:40, :]
    planes0 = [plane_of(s) for s in range(9)]
    for t in range(8):
        value = coef[t, 0:1, :] * planes0[0]
        for s in range(1, 9):
            value += coef[t, s : s + 1, :] * planes0[s]
        refine_own(value, fine0.at[t])
    for c, target, refine in ((1, fine1, refine_wide), (2, fine2, refine_own)):
        planes = [plane_of(2 + 7 * c + s) for s in range(7)]
        for p in range(4):
            value = coef[p + 2, 1:2, :] * planes[0]
            for s in range(1, 7):
                value += coef[p + 2, s + 1 : s + 2, :] * planes[s]
            refine(value, target.at[p])

    def wide(interior, edge, line, columns):
        rest = edge * mix[pl.ds(line, 1), :]
        ah, al = split2(jnp.concatenate([interior, rest], axis=1))
        matrix = rz[:, 0:columns]
        return dot(ah, matrix) + dot(al, matrix)

    flow_z = [wide(fine2[p], edge_own, 18 + p, 384) for p in range(4)]
    flow_z = jnp.concatenate(flow_z, axis=0)
    fh, fl = split2(flow_z[:, 0:256] * theta[...].reshape(128, 256))
    eh, el = split2(flow_z[:, 256:384] * zrecv[...].T)
    total = flow_z[:, 0:256] * gz[...].reshape(128, 256) + along_z(m1h[...], m1l[...], fh, fl, eh, el)
    out_ref[...] = 0.2 * lap[...] - 0.5 * total.reshape(4, 32, 256)
    for p in range(4):
        flow = wide(fine1[p], edge_wide, 10 + p, 256)
        ph, plow = split2(flow * tpad[p])
        slope = dot(my[0:32, 0:144], jnp.concatenate([ph, plow, ph], axis=0))
        own = flow[8:40]
        out_ref[p] -= 0.5 * (own * gy[p] + slope) + own
    flows = [wide(fine0[t], edge_own, t, 256) for t in range(8)]
    flux = [flows[t] * tplane(t) for t in range(8)]
    for i in range(4):
        out_ref[i] -= 0.5 * (flows[i + 2] * gx[i])
    for j in range(4):
        t = j + 2
        one = 28.0 * (flux[t + 1] - flux[t - 1]) + (flux[t + 2] - flux[t - 2])
        for i in range(4):
            out_ref[i] -= (0.5 * (metric[i] * (fx[i, j] * (1.0 / 36.0)))) * one

    for copy in started:
        copy.wait_send()


def local(theta, section, velocity, lower_plane, weight_x, metric_x,
          first_x, first_y, first_z, second_x, second_y, second_z):
    smem = pl.BlockSpec(memory_space=pltpu.SMEM)
    anywhere = pl.BlockSpec(memory_space=pl.ANY)

    def vm(*shape, kind=F32):
        return pltpu.VMEM(shape, kind)

    def sem(n):
        return pltpu.SemaphoreType.DMA((n,))

    tendency = pl.pallas_call(
        kernel,
        out_shape=jax.ShapeDtypeStruct((4, 32, 256), F32),
        in_specs=[smem] * 5 + [anywhere] * 6,
        out_specs=pl.BlockSpec(memory_space=pltpu.VMEM),
        scratch_shapes=[
            vm(4, 32, 256), vm(128, 128), vm(32, 32), vm(32, 32), vm(256, 256), vm(256, 256),
            vm(2, 32, 256), vm(2, 32, 256), vm(8, 128), vm(8, 128), vm(8, 128),
            vm(2, 8, 256), vm(2, 8, 256), vm(2, 8, 128), vm(128, 128), vm(2, 8, 128), vm(2, 8, 128),
            vm(8 * SLAB, 128), vm(24 * SLAB, 128), vm(8, 16, 128), vm(24, 128), vm(256, 384, kind=BF16),
            vm(384, 256, kind=BF16), vm(384, 256, kind=BF16), vm(384, 256, kind=BF16), vm(384, 256, kind=BF16),
            vm(64, 256, kind=BF16), vm(4, 48, 256), vm(24, 128),
            vm(8, 32, 128), vm(4, 48, 128), vm(4, 32, 128), vm(48, 128),
            vm(4, 32, 256), vm(4, 32, 256), vm(4, 32, 256), vm(4, 32, 256),
            sem(6), sem(2), sem(2), sem(2), sem(2), sem(2), sem(2), sem(2), sem(2), sem(2), sem(2),
            sem(7), sem(7), sem(7), sem(7), sem(8), sem(8), sem(2), sem(2),
        ],
        compiler_params=pltpu.CompilerParams(
            collective_id=0, has_side_effects=True, vmem_limit_bytes=32 * 1024 * 1024
        ),
    )(
        lower_plane, weight_x, metric_x, first_x, second_x,
        theta, velocity.reshape(96, 128), first_y, second_y, first_z, second_z,
    )
    section_new = (-5.0 / 9.0) * section + 0.2 * tendency
    theta_new = theta + (15.0 / 16.0) * section_new
    return (theta_new, section_new)


def solution(mesh):
    placed = (
        P("blk", "row", "col"),
        P("blk", "row", "col"),
        P(None, None, ("row", "blk"), "col"),
        P(),
        P("blk"),
        P("blk"),
        P(),
        P(),
        P(),
        P(),
        P(),
        P(),
    )
    return jax.shard_map(
        local,
        mesh=mesh,
        in_specs=placed,
        out_specs=(P("blk", "row", "col"), P("blk", "row", "col")),
        check_vma=False,
    )
```

time: 149 us -> 48.4 us (0.32)
  the two profiles are of different devices: /device:TPU:25 before, /device:TPU:1 now
where the time goes in v1:
time: 48.4 us; the launch traced here: 47.9 us
  Pallas kernels  39.5 us (82%)
  local copies, waits for them, and re-layouts  7.06 us (15%)
  other arithmetic  0.73 us (2%)
  between operations  0.68 us (1%)
    pallas_call x1, Pallas kernels, local(): pl.pallas_call(kernel, out_shape=jax.ShapeDtypeStruct((4, 32, 256), F32),...  39.5 us
    unnamed x24, local copies, waits for them, and re-layouts  7.06 us

profile of v1, /device:TPU:1, one launch (start us, length us, event | category | flops | bytes accessed | tf_op | source)
XLA Modules:
  0.0 47.9 jit_solution(6454909271668953039)
XLA Ops:
  0.6 0.0 copy-start.10
  0.6 0.0 copy-start.9
  0.7 0.0 copy-start.8
  0.7 0.6 %copy-done.10 = f32[4]{0:T(128)S(1)} copy-done((f32[4]{0:T(128)S(1)}, f32[4]{0:T(128)}, u32[]{:S(2)}) %copy-start.10) | copy-done | bytes 40
  1.3 0.0 copy-done.9
  1.3 0.0 copy-done.8
  1.3 0.0 copy-start
  1.3 0.9 %copy-done = f32[4,32,256]{2,1,0:T(8,128)S(1)} copy-done((f32[4,32,256]{2,1,0:T(8,128)S(1)}, f32[4,32,256]{2,1,0:T(8,128)}, u32[]{:S(2)}) %copy-start) | copy-done | bytes 131096
  2.2 0.0 copy-start.1
  2.2 0.9 %copy-done.1 = f32[256,256]{1,0:T(8,128)S(1)} copy-done((f32[256,256]{1,0:T(8,128)S(1)}, f32[256,256]{1,0:T(8,128)}, u32[]{:S(2)}) %copy-start.1) | copy-done | bytes 262168
  3.2 0.0 copy-start.2
  3.2 0.9 %copy-done.2 = f32[256,256]{1,0:T(8,128)S(1)} copy-done((f32[256,256]{1,0:T(8,128)S(1)}, f32[256,256]{1,0:T(8,128)}, u32[]{:S(2)}) %copy-start.2) | copy-done | bytes 262168
  4.1 0.0 copy-start.3
  4.1 0.8 %copy-done.3 = f32[3,32,1,128]{3,2,1,0:T(1,128)S(1)} copy-done((f32[3,32,1,128]{3,2,1,0:T(1,128)S(1)}, f32[3,32,1,128]{3,2,1,0:T(1,128)}, u32[]{:S(2)}) %copy-start.3) | copy-done | bytes 49176
  4.9 0.0 copy-start.4
  4.9 0.7 %copy-done.4 = f32[32,32]{1,0:T(8,128)S(1)} copy-done((f32[32,32]{1,0:T(8,128)S(1)}, f32[32,32]{1,0:T(8,128)}, u32[]{:S(2)}) %copy-start.4) | copy-done | bytes 4120
  5.6 0.0 copy-start.5
  5.6 0.7 %copy-done.5 = f32[32,32]{1,0:T(8,128)S(1)} copy-done((f32[32,32]{1,0:T(8,128)S(1)}, f32[32,32]{1,0:T(8,128)}, u32[]{:S(2)}) %copy-start.5) | copy-done | bytes 4120
  6.4 0.0 copy-start.6
  6.4 0.7 %copy-done.6 = f32[4,4]{1,0:T(4,128)S(1)} copy-done((f32[4,4]{1,0:T(4,128)S(1)}, f32[4,4]{1,0:T(4,128)}, u32[]{:S(2)}) %copy-start.6) | copy-done | bytes 88
  7.0 0.7 %copy-done.7 = f32[4,4]{1,0:T(4,128)S(1)} copy-done((f32[4,4]{1,0:T(4,128)S(1)}, f32[4,4]{1,0:T(4,128)}, u32[]{:S(2)}) %copy-start.7) | copy-done | bytes 88
  7.7 39.5 %shard_map.131 = f32[4,32,256]{2,1,0:T(8,128)S(1)} custom-call(s32[64]{0:T(128)S(1)} %copy-done.8, f32[4]{0:T(128)S(1)} %copy-done.9, f32[4]{0:T(128)S(1)} %copy-done.10, f32[4,4]{1,0:T(4,128)S(1)} %copy-done.6, f32[4,4]{1,0:T(4,128)S(1)} %copy-done.7, f32[4,32,256]{2,1,0:T(8,128)S(1)} %copy-done, f32[96,128]{1,0:T(8,128)S(1)} %bitcast.1, ...), custom_call_target="tpu_custom_call" | custom-call | tf_op jit(solution)/shard_map/pallas_call | solution.py:385
  47.2 0.0 copy-done.11
  47.2 0.7 %multiply_add_fusion = (f32[4,32,256]{2,1,0:T(8,128)}, f32[4,32,256]{2,1,0:T(8,128)}) fusion(f32[4,32,256]{2,1,0:T(8,128)S(1)} %copy-done, f32[4,32,256]{2,1,0:T(8,128)S(1)} %shard_map.131, f32[4,32,256]{2,1,0:T(8,128)S(1)} %copy-done.11), kind=kLoop, calls=%fused_computation | loop fusion | flops 163840 | bytes 655360 | tf_op jit(solution)/shard_map/add | solution.py:410
  (2 shorter events, 0.0 us)
Async XLA Ops:
  0.6 0.7 %copy-start.10 = (f32[4]{0:T(128)S(1)}, f32[4]{0:T(128)}, u32[]{:S(2)}) copy-start(f32[4]{0:T(128)} %metric.1) | copy-start | bytes 52
  0.6 0.7 %copy-start.9 = (f32[4]{0:T(128)S(1)}, f32[4]{0:T(128)}, u32[]{:S(2)}) copy-start(f32[4]{0:T(128)} %weight.1) | copy-start | bytes 52
  0.7 0.7 %copy-start.8 = (s32[64]{0:T(128)S(1)}, s32[64]{0:T(128)}, u32[]{:S(2)}) copy-start(s32[64]{0:T(128)} %lower.1) | copy-start | bytes 772
  1.3 0.9 %copy-start = (f32[4,32,256]{2,1,0:T(8,128)S(1)}, f32[4,32,256]{2,1,0:T(8,128)}, u32[]{:S(2)}) copy-start(f32[4,32,256]{2,1,0:T(8,128)} %theta_in.1) | copy-start | bytes 393220
  2.2 0.9 %copy-start.1 = (f32[256,256]{1,0:T(8,128)S(1)}, f32[256,256]{1,0:T(8,128)}, u32[]{:S(2)}) copy-start(f32[256,256]{1,0:T(8,128)} %fz_in.1) | copy-start | bytes 786436
  3.2 0.9 %copy-start.2 = (f32[256,256]{1,0:T(8,128)S(1)}, f32[256,256]{1,0:T(8,128)}, u32[]{:S(2)}) copy-start(f32[256,256]{1,0:T(8,128)} %sz_in.1) | copy-start | bytes 786436
  4.1 0.8 %copy-start.3 = (f32[3,32,1,128]{3,2,1,0:T(1,128)S(1)}, f32[3,32,1,128]{3,2,1,0:T(1,128)}, u32[]{:S(2)}) copy-start(f32[3,32,1,128]{3,2,1,0:T(1,128)} %param.14) | copy-start | bytes 147460
  4.9 0.7 %copy-start.4 = (f32[32,32]{1,0:T(8,128)S(1)}, f32[32,32]{1,0:T(8,128)}, u32[]{:S(2)}) copy-start(f32[32,32]{1,0:T(8,128)} %fy_in.1) | copy-start | bytes 12292
  5.6 0.7 %copy-start.5 = (f32[32,32]{1,0:T(8,128)S(1)}, f32[32,32]{1,0:T(8,128)}, u32[]{:S(2)}) copy-start(f32[32,32]{1,0:T(8,128)} %sy_in.1) | copy-start | bytes 12292
  6.4 0.7 %copy-start.6 = (f32[4,4]{1,0:T(4,128)S(1)}, f32[4,4]{1,0:T(4,128)}, u32[]{:S(2)}) copy-start(f32[4,4]{1,0:T(4,128)} %fx.1) | copy-start | bytes 196
  7.0 0.7 %copy-start.7 = (f32[4,4]{1,0:T(4,128)S(1)}, f32[4,4]{1,0:T(4,128)}, u32[]{:S(2)}) copy-start(f32[4,4]{1,0:T(4,128)} %sx.1) | copy-start | bytes 196
  7.7 39.5 %copy-start.11 = (f32[4,32,256]{2,1,0:T(8,128)S(1)}, f32[4,32,256]{2,1,0:T(8,128)}, u32[]{:S(2)}) copy-start(f32[4,32,256]{2,1,0:T(8,128)} %param.13) | copy-start | bytes 393220

commit v2 on v1

--- a/solution.py
+++ b/solution.py
@@ -56,7 +56,7 @@
     pack, buf, coef, mix, rz, m1h, m1l, m2h, m2l, my, tpad, vt, fine0, fine1, fine2, efine,
     gx, gy, gz, lap,
     in_sem, x_send, x_recv, w_send, w_recv, y_send, y_recv, z_send, z_recv, v_send, v_recv,
-    a_send, a_recv, b_send, b_recv, p_send, p_recv, r_send, r_recv,
+    a_send, a_recv, p_send, p_recv, r_send, r_recv, h_send,
 ):
     row, col, blk = lax.axis_index("row"), lax.axis_index("col"), lax.axis_index("blk")
     rows, cols = lax.axis_size("row"), lax.axis_size("col")
@@ -72,7 +72,6 @@
         loads.append(load)
 
     partner = {"blk": 2 * chip + (1 - core)}
-    outer = {"blk": (blk + 2 * core + 15) % 16}
     up_blk, down_blk = {"blk": (blk + 1) % 16}, {"blk": (blk + 15) % 16}
     up_row, down_row = {"row": (row + 1) % rows}, {"row": (row + rows - 1) % rows}
     up_col, down_col = {"col": (col + 1) % cols}, {"col": (col + cols - 1) % cols}
@@ -82,9 +81,28 @@
         senders.append(((zhi + far) % 2) * 4 + (ypos + 4 - dy) % 4)
 
     barrier = pltpu.get_barrier_semaphore()
-    peers = [{"blk": 2 * q + core} for q in chips] + [partner, outer, up_row, down_row, up_col, down_col]
+    outer = {"blk": (blk + 2 * core + 15) % 16}
+    peers = [{"blk": 2 * q + core} for q in chips] + [partner, outer, up_col, down_col]
+    peers += [up_row, down_row, {**up_row, **partner}, {**down_row, **partner}]
     for peer in peers:
         pl.semaphore_signal(barrier, inc=1, device_id=peer, device_id_type=pl.DeviceIdType.MESH)
+    near_row = jnp.where(zhi == 0, up_row["row"], down_row["row"])
+    edge_row = jnp.where(zhi == 0, down_row["row"], up_row["row"])
+    at_edge = row == jnp.where(zhi == 0, 0, rows - 1)
+    for n in (0, 1):
+        owner = {"row": near_row, "blk": 14 * zhi + n}
+        pl.semaphore_signal(barrier, inc=1, device_id=owner, device_id_type=pl.DeviceIdType.MESH)
+
+    @pl.when(at_edge)
+    def _():
+        for n in (0, 1):
+            owner = {"row": edge_row, "blk": 14 * (1 - zhi) + n}
+            pl.semaphore_signal(barrier, inc=1, device_id=owner, device_id_type=pl.DeviceIdType.MESH)
+
+    owns = (blk <= 1) | (blk >= 14)
+    to_row = jnp.where(zhi == 0, down_row["row"], up_row["row"])
+    owns_all = owns & (row == jnp.where(zhi == 0, 0, rows - 1))
+    expected = len(peers) + jnp.where(owns, 8, 0) + jnp.where(owns_all, 8, 0)
 
     started = []
 
@@ -104,6 +122,19 @@
 
     vel[pl.ds(96, 32), :] = jnp.zeros((32, 128), F32)
     loads[0].wait()
+    vel_t = vel[...].T
+    vzpack[0] = vel_t[0:8]
+    vzpack[1] = vel_t[120:128]
+    def slot(b):
+        return pl.ds(pl.multiple_of((b + 2) * SLAB, 8), SLAB)
+
+    def part(first, offset, count):
+        return pl.ds(pl.multiple_of(first + offset, 8), count)
+
+    pl.semaphore_wait(barrier, expected)
+
+    send(vzpack.at[1], vzrecv.at[0], v_send.at[0], v_recv.at[0], up_col)
+    send(vzpack.at[0], vzrecv.at[1], v_send.at[1], v_recv.at[1], down_col)
     for q in range(8):
         for base, comp, first, count in ((0, 0, 4 * q - 2, 9), (9, 1, 4 * q - 1, 7), (16, 2, 4 * q - 1, 7)):
             at = 0
@@ -112,41 +143,21 @@
                 take = min(count - at, 32 - plane)
                 pack[pl.ds(q * SLAB + base + at, take), :] = vel[pl.ds(comp * 32 + plane, take), :]
                 at += take
-    vel_t = vel[...].T
-    vzpack[0] = vel_t[0:8]
-    vzpack[1] = vel_t[120:128]
     loads[1].wait()
     for p in range(4):
         ypack[0, pl.ds(2 * p, 2), :] = theta[p, 0:2, :]
         ypack[1, pl.ds(2 * p, 2), :] = theta[p, 30:32, :]
-    zpack[0] = theta[:, :, 0:128].reshape(128, 128).T[0:8]
-    zpack[1] = theta[:, :, 128:256].reshape(128, 128).T[120:128]
+    send(ypack.at[1], yrecv.at[0], y_send.at[0], y_recv.at[0], up_row)
+    send(ypack.at[0], yrecv.at[1], y_send.at[1], y_recv.at[1], down_row)
+    send(theta.at[pl.ds(2, 2)], xlo, x_send.at[0], x_recv.at[0], up_blk)
+    send(theta.at[pl.ds(0, 2)], xhi, x_send.at[1], x_recv.at[1], down_blk)
     wown[...] = jnp.concatenate(
         [jnp.full((1, 128), weight[p], F32) for p in range(4)] + [jnp.zeros((4, 128), F32)], axis=0
     )
-
-    def slot(b):
-        return pl.ds(pl.multiple_of((b + 2) * SLAB, 8), SLAB)
-
-    def part(first, offset, count):
-        return pl.ds(pl.multiple_of(first + offset, 8), count)
-
-    pl.semaphore_wait(barrier, len(peers))
-
-    send(vzpack.at[1], vzrecv.at[0], v_send.at[0], v_recv.at[0], up_col)
-    send(vzpack.at[0], vzrecv.at[1], v_send.at[1], v_recv.at[1], down_col)
-    land = (blk + 2) * SLAB
-    for n, q in enumerate(chips):
-        send(
-            pack.at[part(q * SLAB, 0, 16)], buf.at[part(land, 0, 16)],
-            a_send.at[n], a_recv.at[n], {"blk": 2 * q + core},
-        )
-    send(theta.at[pl.ds(2, 2)], xlo, x_send.at[0], x_recv.at[0], up_blk)
-    send(theta.at[pl.ds(0, 2)], xhi, x_send.at[1], x_recv.at[1], down_blk)
     send(wown, wlo, w_send.at[0], w_recv.at[0], up_blk)
     send(wown, whi, w_send.at[1], w_recv.at[1], down_blk)
-    send(ypack.at[1], yrecv.at[0], y_send.at[0], y_recv.at[0], up_row)
-    send(ypack.at[0], yrecv.at[1], y_send.at[1], y_recv.at[1], down_row)
+    zpack[0] = theta[:, :, 0:128].reshape(128, 128).T[0:8]
+    zpack[1] = theta[:, :, 128:256].reshape(128, 128).T[120:128]
     send(zpack.at[1], zrecv.at[pl.ds(0, 8)], z_send.at[0], z_recv.at[0], up_col)
     send(zpack.at[0], zrecv.at[pl.ds(8, 8)], z_send.at[1], z_recv.at[1], down_col)
 
@@ -178,12 +189,59 @@
         edge_rows = jnp.where(lane8 == e, picked[8 * e : 8 * e + 8], edge_rows)
     for q in range(8):
         pack[pl.ds(q * SLAB + 23, 1), :] = edge_rows[q : q + 1]
+    own_slab = pl.ds(pl.multiple_of(chip * SLAB, 8), SLAB)
+
+    def row_copies(src, side):
+        device, place, which = ((up_row, core, core), (down_row, core + 18, core + 2))[side]
+        return [
+            pltpu.make_async_remote_copy(
+                src_ref=src, dst_ref=buf.at[part(place * SLAB, 0, SLAB)],
+                send_sem=r_send.at[2 * side + n], recv_sem=r_recv.at[which],
+                device_id=where, device_id_type=pl.DeviceIdType.MESH,
+            )
+            for n, where in enumerate((device, {**device, **partner}))
+        ]
+
+    forward_up, forward_down = (zhi == 0) & (row < rows - 1), (zhi == 1) & (row > 0)
+
+    def pass_on(src, q):
+        @pl.when((q == 7) & forward_up)
+        def _():
+            for copy in row_copies(src, 0):
+                copy.start()
+
+        @pl.when((q == 0) & forward_down)
+        def _():
+            for copy in row_copies(src, 1):
+                copy.start()
+
+    def owner_copies(half):
+        place = jnp.where(zhi == 0, 18, 0) + core
+        copies = []
+        for n in range(8):
+            b = 8 * half + n
+            copies.append(pltpu.make_async_remote_copy(
+                src_ref=pack.at[part((b // 2) * SLAB, 0, SLAB)], dst_ref=buf.at[part(place * SLAB, 0, SLAB)],
+                send_sem=h_send.at[b], recv_sem=r_recv.at[jnp.where(zhi == 0, 2, 0) + core],
+                device_id={"row": to_row, "blk": b}, device_id_type=pl.DeviceIdType.MESH,
+            ))
+        return copies
+
     for n, q in enumerate(chips):
         send(
-            pack.at[part(q * SLAB, 16, 8)], buf.at[part(land, 16, 8)],
-            b_send.at[n], b_recv.at[n], {"blk": 2 * q + core},
+            pack.at[part(q * SLAB, 0, SLAB)], buf.at[slot(blk)], a_send.at[n], a_recv.at[n], {"blk": 2 * q + core}
         )
-    own_slab = pl.ds(pl.multiple_of(chip * SLAB, 8), SLAB)
+    @pl.when(owns)
+    def _():
+        for copy in owner_copies(zhi):
+            copy.start()
+
+    @pl.when(owns_all)
+    def _():
+        for copy in owner_copies(1 - zhi):
+            copy.start()
+
+    pass_on(pack.at[own_slab], chip)
     send(pack.at[own_slab], buf.at[slot(blk)], p_send.at[7], p_recv.at[7], partner)
     buf[slot(blk), :] = pack[own_slab, :]
 
@@ -240,13 +298,6 @@
         gy[p] = res[0:32]
         lap[p] += res[32:64]
 
-    for n, q in enumerate(senders):
-        b = 2 * q + core
-        first = (b + 2) * SLAB
-        arrived(buf.at[part(first, 0, 16)], a_send.at[n], a_recv.at[n], {"blk": b})
-        arrived(buf.at[part(first, 16, 8)], b_send.at[n], b_recv.at[n], {"blk": b})
-        send(buf.at[slot(b)], buf.at[slot(b)], p_send.at[n], p_recv.at[n], partner)
-
     arrived(wlo, w_send.at[0], w_recv.at[0], down_blk)
     arrived(whi, w_send.at[1], w_recv.at[1], up_blk)
     s_row = iota((16, 128), 0)
@@ -294,20 +345,22 @@
                 gx[i] += s1 * one
             lap[i] += s2 * two
 
-    for n, q in enumerate(senders):
-        b = 2 * q + 1 - core
-        arrived(buf.at[slot(b)], p_send.at[n], p_recv.at[n], partner)
-    arrived(buf.at[slot(2 * chip + 1 - core)], p_send.at[7], p_recv.at[7], partner)
-    send(buf.at[pl.ds(16 * SLAB, 2 * SLAB)], buf.at[pl.ds(0, 2 * SLAB)], r_send.at[0], r_recv.at[0], up_row)
-    send(buf.at[pl.ds(2 * SLAB, 2 * SLAB)], buf.at[pl.ds(18 * SLAB, 2 * SLAB)], r_send.at[1], r_recv.at[1], down_row)
     buf[pl.ds(20 * SLAB, 4 * SLAB), :] = jnp.zeros((4 * SLAB, 128), F32)
     for p in range(4):
         fine1[p, 0:8, :] = jnp.zeros((8, 128), F32)
         fine1[p, 40:48, :] = jnp.zeros((8, 128), F32)
     efine[0:8, :] = jnp.zeros((8, 128), F32)
     efine[40:48, :] = jnp.zeros((8, 128), F32)
-    arrived(buf.at[pl.ds(0, 2 * SLAB)], r_send.at[0], r_recv.at[0], down_row)
-    arrived(buf.at[pl.ds(18 * SLAB, 2 * SLAB)], r_send.at[1], r_recv.at[1], up_row)
+    for n in (4, 5, 6, 0, 1, 2, 3):
+        b = 2 * senders[n] + core
+        arrived(buf.at[slot(b)], a_send.at[n], a_recv.at[n], {"blk": b})
+        pass_on(buf.at[slot(b)], senders[n])
+        send(buf.at[slot(b)], buf.at[slot(b)], p_send.at[n], p_recv.at[n], partner)
+    for n, q in enumerate(senders):
+        arrived(buf.at[slot(2 * q + 1 - core)], p_send.at[n], p_recv.at[n], partner)
+    arrived(buf.at[slot(2 * chip + 1 - core)], p_send.at[7], p_recv.at[7], partner)
+    for n, place in enumerate((0, 1, 18, 19)):
+        arrived(buf.at[pl.ds(place * SLAB, SLAB)], r_send.at[n], r_recv.at[n], up_row)
 
     def plane_of(line):
         return buf[pl.ds(line, 24, stride=SLAB), :]
@@ -370,11 +423,27 @@
     for copy in started:
         copy.wait_send()
 
+    for side, used in ((0, forward_up), (1, forward_down)):
+        @pl.when(used)
+        def _(side=side):
+            for copy in row_copies(buf.at[pl.ds(0, SLAB)], side):
+                copy.wait_send()
+
+    @pl.when(owns)
+    def _():
+        for copy in owner_copies(zhi):
+            copy.wait_send()
+
+    @pl.when(owns_all)
+    def _():
+        for copy in owner_copies(1 - zhi):
+            copy.wait_send()
+
 
 def local(theta, section, velocity, lower_plane, weight_x, metric_x,
           first_x, first_y, first_z, second_x, second_y, second_z):
     smem = pl.BlockSpec(memory_space=pltpu.SMEM)
-    anywhere = pl.BlockSpec(memory_space=pl.ANY)
+    anywhere = pl.BlockSpec(memory_space=pltpu.HBM)
 
     def vm(*shape, kind=F32):
         return pltpu.VMEM(shape, kind)
@@ -384,7 +453,7 @@
 
     tendency = pl.pallas_call(
         kernel,
-        out_shape=jax.ShapeDtypeStruct((4, 32, 256), F32),
+        out_shape=pltpu.VMEM((4, 32, 256), F32),
         in_specs=[smem] * 5 + [anywhere] * 6,
         out_specs=pl.BlockSpec(memory_space=pltpu.VMEM),
         scratch_shapes=[
@@ -397,10 +466,10 @@
             vm(8, 32, 128), vm(4, 48, 128), vm(4, 32, 128), vm(48, 128),
             vm(4, 32, 256), vm(4, 32, 256), vm(4, 32, 256), vm(4, 32, 256),
             sem(6), sem(2), sem(2), sem(2), sem(2), sem(2), sem(2), sem(2), sem(2), sem(2), sem(2),
-            sem(7), sem(7), sem(7), sem(7), sem(8), sem(8), sem(2), sem(2),
+            sem(7), sem(7), sem(8), sem(8), sem(4), sem(4), sem(16),
         ],
         compiler_params=pltpu.CompilerParams(
-            collective_id=0, has_side_effects=True, vmem_limit_bytes=32 * 1024 * 1024
+            collective_id=0, has_side_effects=True, vmem_limit_bytes=60 * 1024 * 1024
         ),
     )(
         lower_plane, weight_x, metric_x, first_x, second_x,

time: 48.4 us -> 34.9 us (0.72)
  local copies, waits for them, and re-layouts: 7.06 us -> 0.01 us
  Pallas kernels: 39.5 us -> 33.3 us
    unnamed x24 -> x4, local copies, waits for them, and re-layouts: 7.06 us -> 0.01 us
    pallas_call x1, Pallas kernels: 39.5 us -> 33.3 us  [local(): pl.pallas_call(kernel, out_shape=pltpu.VMEM((4, 32, 256), F32), in_specs=...]
where the time goes in v2:
time: 34.9 us; the launch traced here: 34.7 us
  Pallas kernels  33.3 us (95%)
  other arithmetic  0.73 us (2%)
  between operations  0.67 us (2%)
    pallas_call x1, Pallas kernels, local(): pl.pallas_call(kernel, out_shape=pltpu.VMEM((4, 32, 256), F32), in_specs=...  33.3 us
    add x1, other arithmetic, local(): theta_new = theta + 15.0 / 16.0 * section_new  0.73 us

profile of v2, /device:TPU:1, one launch (start us, length us, event | category | flops | bytes accessed | tf_op | source)
XLA Modules:
  0.0 34.7 jit_solution(5949414514045986716)
XLA Ops:
  0.6 0.0 copy-start
  0.6 0.0 copy-start.1
  0.7 33.3 %shard_map.131 = f32[4,32,256]{2,1,0:T(8,128)S(1)} custom-call(s32[64]{0:T(128)} %lower.1, f32[4]{0:T(128)} %weight.1, f32[4]{0:T(128)} %metric.1, f32[4,4]{1,0:T(4,128)} %fx.1, f32[4,4]{1,0:T(4,128)} %sx.1, f32[4,32,256]{2,1,0:T(8,128)} %theta_in.1, f32[96,128]{1,0:T(8,128)} %bitcast.1, f32[32,32]{1,0:T(8,128)} %fy_in.1, f32[32,32]{1,0:T(8,128)} %sy_in.1, ...), custom_call_target="tpu_custom_call" | custom-call | tf_op jit(solution)/shard_map/pallas_call | solution.py:454
  34.0 0.0 copy-done
  34.0 0.0 copy-done.1
  34.0 0.7 %multiply_add_fusion = (f32[4,32,256]{2,1,0:T(8,128)}, f32[4,32,256]{2,1,0:T(8,128)}) fusion(f32[4,32,256]{2,1,0:T(8,128)S(1)} %copy-done, f32[4,32,256]{2,1,0:T(8,128)S(1)} %shard_map.131, f32[4,32,256]{2,1,0:T(8,128)S(1)} %copy-done.1), kind=kLoop, calls=%fused_computation | loop fusion | flops 163840 | bytes 655360 | tf_op jit(solution)/shard_map/add | solution.py:479
Async XLA Ops:
  0.6 33.3 %copy-start = (f32[4,32,256]{2,1,0:T(8,128)S(1)}, f32[4,32,256]{2,1,0:T(8,128)}, u32[]{:S(2)}) copy-start(f32[4,32,256]{2,1,0:T(8,128)} %theta_in.1) | copy-start | bytes 393220
  0.6 33.3 %copy-start.1 = (f32[4,32,256]{2,1,0:T(8,128)S(1)}, f32[4,32,256]{2,1,0:T(8,128)}, u32[]{:S(2)}) copy-start(f32[4,32,256]{2,1,0:T(8,128)} %param.13) | copy-start | bytes 393220

commit v3 on v2

--- a/solution.py
+++ b/solution.py
@@ -123,18 +123,25 @@
     vel[pl.ds(96, 32), :] = jnp.zeros((32, 128), F32)
     loads[0].wait()
     vel_t = vel[...].T
-    vzpack[0] = vel_t[0:8]
-    vzpack[1] = vel_t[120:128]
-    def slot(b):
-        return pl.ds(pl.multiple_of((b + 2) * SLAB, 8), SLAB)
-
-    def part(first, offset, count):
-        return pl.ds(pl.multiple_of(first + offset, 8), count)
-
-    pl.semaphore_wait(barrier, expected)
-
-    send(vzpack.at[1], vzrecv.at[0], v_send.at[0], v_recv.at[0], up_col)
-    send(vzpack.at[0], vzrecv.at[1], v_send.at[1], v_recv.at[1], down_col)
+    p_row, l_col = iota((128, 128), 0), iota((128, 128), 1)
+    plane = p_row & 31
+    comp = p_row >> 5
+    place = jnp.where(comp == 0, plane & 15, jnp.where(comp == 1, 16 + (plane & 7), 24 + (plane & 7)))
+    select = jnp.where((place == (l_col & 31)) & (comp < 3), 1.0, 0.0).astype(BF16)
+    k_row, p_lane = iota((8, 128), 0), iota((8, 128), 1)
+    plane8 = p_lane & 31
+    inside0 = ((plane8 - 4 * k_row + 34) & 31) < 9
+    inside1 = ((plane8 - 4 * k_row + 33) & 31) < 7
+    lead = p_lane < 32
+    window = (lead & inside0) | (jnp.logical_not(lead) & inside1)
+    edges = jnp.concatenate(
+        [jnp.where(window, jnp.broadcast_to(vel_t[e : e + 1], (8, 128)), 0.0) for e in (0, 1, 126, 127)], axis=0
+    )
+    picked = sum(dot(piece, select) for piece in split3(edges))
+    lane8 = iota((8, 128), 1) >> 5
+    nothing = jnp.zeros((8, 128), F32)
+    vzpack[0] = jnp.where(lane8 == 2, picked[0:8], jnp.where(lane8 == 3, picked[8:16], nothing))
+    vzpack[1] = jnp.where(lane8 == 0, picked[16:24], jnp.where(lane8 == 1, picked[24:32], nothing))
     for q in range(8):
         for base, comp, first, count in ((0, 0, 4 * q - 2, 9), (9, 1, 4 * q - 1, 7), (16, 2, 4 * q - 1, 7)):
             at = 0
@@ -147,6 +154,17 @@
     for p in range(4):
         ypack[0, pl.ds(2 * p, 2), :] = theta[p, 0:2, :]
         ypack[1, pl.ds(2 * p, 2), :] = theta[p, 30:32, :]
+
+    def slot(b):
+        return pl.ds(pl.multiple_of((b + 2) * SLAB, 8), SLAB)
+
+    def part(first, offset, count):
+        return pl.ds(pl.multiple_of(first + offset, 8), count)
+
+    pl.semaphore_wait(barrier, expected)
+
+    send(vzpack.at[1], vzrecv.at[0], v_send.at[0], v_recv.at[0], up_col)
+    send(vzpack.at[0], vzrecv.at[1], v_send.at[1], v_recv.at[1], down_col)
     send(ypack.at[1], yrecv.at[0], y_send.at[0], y_recv.at[0], up_row)
     send(ypack.at[0], yrecv.at[1], y_send.at[1], y_recv.at[1], down_row)
     send(theta.at[pl.ds(2, 2)], xlo, x_send.at[0], x_recv.at[0], up_blk)
@@ -161,34 +179,12 @@
     send(zpack.at[1], zrecv.at[pl.ds(0, 8)], z_send.at[0], z_recv.at[0], up_col)
     send(zpack.at[0], zrecv.at[pl.ds(8, 8)], z_send.at[1], z_recv.at[1], down_col)
 
-    p_row, l_col = iota((128, 128), 0), iota((128, 128), 1)
-    plane = p_row & 31
-    comp = p_row >> 5
-    place = jnp.where(comp == 0, plane & 15, jnp.where(comp == 1, 16 + (plane & 7), 24 + (plane & 7)))
-    select = jnp.where((place == (l_col & 31)) & (comp < 3), 1.0, 0.0).astype(BF16)
-    k_row, p_lane = iota((8, 128), 0), iota((8, 128), 1)
-    plane8 = p_lane & 31
-    inside0 = ((plane8 - 4 * k_row + 34) & 31) < 9
-    inside1 = ((plane8 - 4 * k_row + 33) & 31) < 7
-    lead = p_lane < 32
-    window = (lead & inside0) | (jnp.logical_not(lead) & inside1)
     arrived(vzrecv.at[0], v_send.at[0], v_recv.at[0], down_col)
     arrived(vzrecv.at[1], v_send.at[1], v_recv.at[1], up_col)
-    left, right = vzrecv[0], vzrecv[1]
-    edges = jnp.concatenate(
-        [
-            jnp.where(window, jnp.broadcast_to(one, (8, 128)), 0.0)
-            for one in (left[6:7], left[7:8], right[0:1], right[1:2])
-        ],
-        axis=0,
-    )
-    picked = sum(dot(piece, select) for piece in split3(edges))
-    lane8 = iota((8, 128), 1) >> 5
-    edge_rows = jnp.zeros((8, 128), F32)
-    for e in range(4):
-        edge_rows = jnp.where(lane8 == e, picked[8 * e : 8 * e + 8], edge_rows)
+    edge_rows = vzrecv[0] + vzrecv[1]
     for q in range(8):
         pack[pl.ds(q * SLAB + 23, 1), :] = edge_rows[q : q + 1]
+
     own_slab = pl.ds(pl.multiple_of(chip * SLAB, 8), SLAB)
 
     def row_copies(src, side):
@@ -298,6 +294,11 @@
         gy[p] = res[0:32]
         lap[p] += res[32:64]
 
+    for n in (4, 5, 6, 0, 1, 2, 3):
+        b = 2 * senders[n] + core
+        arrived(buf.at[slot(b)], a_send.at[n], a_recv.at[n], {"blk": b})
+        pass_on(buf.at[slot(b)], senders[n])
+        send(buf.at[slot(b)], buf.at[slot(b)], p_send.at[n], p_recv.at[n], partner)
     arrived(wlo, w_send.at[0], w_recv.at[0], down_blk)
     arrived(whi, w_send.at[1], w_recv.at[1], up_blk)
     s_row = iota((16, 128), 0)
@@ -351,11 +352,6 @@
         fine1[p, 40:48, :] = jnp.zeros((8, 128), F32)
     efine[0:8, :] = jnp.zeros((8, 128), F32)
     efine[40:48, :] = jnp.zeros((8, 128), F32)
-    for n in (4, 5, 6, 0, 1, 2, 3):
-        b = 2 * senders[n] + core
-        arrived(buf.at[slot(b)], a_send.at[n], a_recv.at[n], {"blk": b})
-        pass_on(buf.at[slot(b)], senders[n])
-        send(buf.at[slot(b)], buf.at[slot(b)], p_send.at[n], p_recv.at[n], partner)
     for n, q in enumerate(senders):
         arrived(buf.at[slot(2 * q + 1 - core)], p_send.at[n], p_recv.at[n], partner)
     arrived(buf.at[slot(2 * chip + 1 - core)], p_send.at[7], p_recv.at[7], partner)
@@ -392,25 +388,26 @@
                 value += coef[p + 2, s + 1 : s + 2, :] * planes[s]
             refine(value, target.at[p])
 
-    def wide(interior, edge, line, columns):
-        rest = edge * mix[pl.ds(line, 1), :]
-        ah, al = split2(jnp.concatenate([interior, rest], axis=1))
-        matrix = rz[:, 0:columns]
-        return dot(ah, matrix) + dot(al, matrix)
-
-    flow_z = [wide(fine2[p], edge_own, 18 + p, 384) for p in range(4)]
-    flow_z = jnp.concatenate(flow_z, axis=0)
-    fh, fl = split2(flow_z[:, 0:256] * theta[...].reshape(128, 256))
-    eh, el = split2(flow_z[:, 256:384] * zrecv[...].T)
-    total = flow_z[:, 0:256] * gz[...].reshape(128, 256) + along_z(m1h[...], m1l[...], fh, fl, eh, el)
+    lines = [(fine2[p], edge_own, 18 + p) for p in range(4)]
+    lines += [(fine1[p], edge_wide, 10 + p) for p in range(4)]
+    lines += [(fine0[t], edge_own, t) for t in range(8)]
+    interior = jnp.concatenate([one for one, _, _ in lines], axis=0)
+    sides = jnp.concatenate([edge * mix[pl.ds(line, 1), :] for _, edge, line in lines], axis=0)
+    xh, xl = split2(jnp.concatenate([interior, sides], axis=1))
+    flow = dot(xh, rz[:, 0:256]) + dot(xl, rz[:, 0:256])
+    flow_side = dot(xh[0:128], rz[:, 256:384]) + dot(xl[0:128], rz[:, 256:384])
+
+    fh, fl = split2(flow[0:128] * theta[...].reshape(128, 256))
+    eh, el = split2(flow_side * zrecv[...].T)
+    total = flow[0:128] * gz[...].reshape(128, 256) + along_z(m1h[...], m1l[...], fh, fl, eh, el)
     out_ref[...] = 0.2 * lap[...] - 0.5 * total.reshape(4, 32, 256)
     for p in range(4):
-        flow = wide(fine1[p], edge_wide, 10 + p, 256)
-        ph, plow = split2(flow * tpad[p])
+        flow_y = flow[128 + 48 * p : 176 + 48 * p]
+        ph, plow = split2(flow_y * tpad[p])
         slope = dot(my[0:32, 0:144], jnp.concatenate([ph, plow, ph], axis=0))
-        own = flow[8:40]
+        own = flow_y[8:40]
         out_ref[p] -= 0.5 * (own * gy[p] + slope) + own
-    flows = [wide(fine0[t], edge_own, t, 256) for t in range(8)]
+    flows = [flow[320 + 32 * t : 352 + 32 * t] for t in range(8)]
     flux = [flows[t] * tplane(t) for t in range(8)]
     for i in range(4):
         out_ref[i] -= 0.5 * (flows[i + 2] * gx[i])

time: 34.9 us -> 33.9 us (0.971)
  Pallas kernels: 33.3 us -> 32.3 us
    pallas_call x1, Pallas kernels: 33.3 us -> 32.3 us  [local(): pl.pallas_call(kernel, out_shape=pltpu.VMEM((4, 32, 256), F32), in_specs=...]
where the time goes in v3:
time: 33.9 us; the launch traced here: 33.7 us
  Pallas kernels  32.3 us (95%)
  other arithmetic  0.73 us (2%)
  between operations  0.67 us (2%)
    pallas_call x1, Pallas kernels, local(): pl.pallas_call(kernel, out_shape=pltpu.VMEM((4, 32, 256), F32), in_specs=...  32.3 us
    add x1, other arithmetic, local(): theta_new = theta + 15.0 / 16.0 * section_new  0.73 us

profile of v3, /device:TPU:1, one launch (start us, length us, event | category | flops | bytes accessed | tf_op | source)
XLA Modules:
  0.0 33.7 jit_solution(8218965392407729498)
XLA Ops:
  0.6 0.0 copy-start
  0.6 0.0 copy-start.1
  0.7 32.3 %shard_map.131 = f32[4,32,256]{2,1,0:T(8,128)S(1)} custom-call(s32[64]{0:T(128)} %lower.1, f32[4]{0:T(128)} %weight.1, f32[4]{0:T(128)} %metric.1, f32[4,4]{1,0:T(4,128)} %fx.1, f32[4,4]{1,0:T(4,128)} %sx.1, f32[4,32,256]{2,1,0:T(8,128)} %theta_in.1, f32[96,128]{1,0:T(8,128)} %bitcast.1, f32[32,32]{1,0:T(8,128)} %fy_in.1, f32[32,32]{1,0:T(8,128)} %sy_in.1, ...), custom_call_target="tpu_custom_call" | custom-call | tf_op jit(solution)/shard_map/pallas_call | solution.py:451
  33.0 0.0 copy-done
  33.0 0.0 copy-done.1
  33.0 0.7 %multiply_add_fusion = (f32[4,32,256]{2,1,0:T(8,128)}, f32[4,32,256]{2,1,0:T(8,128)}) fusion(f32[4,32,256]{2,1,0:T(8,128)S(1)} %copy-done, f32[4,32,256]{2,1,0:T(8,128)S(1)} %shard_map.131, f32[4,32,256]{2,1,0:T(8,128)S(1)} %copy-done.1), kind=kLoop, calls=%fused_computation | loop fusion | flops 163840 | bytes 655360 | tf_op jit(solution)/shard_map/add | solution.py:476
Async XLA Ops:
  0.6 32.4 %copy-start = (f32[4,32,256]{2,1,0:T(8,128)S(1)}, f32[4,32,256]{2,1,0:T(8,128)}, u32[]{:S(2)}) copy-start(f32[4,32,256]{2,1,0:T(8,128)} %theta_in.1) | copy-start | bytes 393220
  0.6 32.4 %copy-start.1 = (f32[4,32,256]{2,1,0:T(8,128)S(1)}, f32[4,32,256]{2,1,0:T(8,128)}, u32[]{:S(2)}) copy-start(f32[4,32,256]{2,1,0:T(8,128)} %param.13) | copy-start | bytes 393220

commit v4 on v3

--- a/solution.py
+++ b/solution.py
@@ -267,6 +267,11 @@
     other = near + 2 * (zz & 1) - 1
     rz[...] = jnp.where(cell == near, 0.75, jnp.where(cell == other, 0.25, jnp.zeros((256, 384), F32))).astype(BF16)
 
+    for n in (4, 5, 6):
+        b = 2 * senders[n] + core
+        arrived(buf.at[slot(b)], a_send.at[n], a_recv.at[n], {"blk": b})
+        pass_on(buf.at[slot(b)], senders[n])
+        send(buf.at[slot(b)], buf.at[slot(b)], p_send.at[n], p_recv.at[n], partner)
     zrecv[pl.ds(16, 112), :] = jnp.zeros((112, 128), F32)
     for p in range(4):
         tpad[p, 0:8, :] = jnp.zeros((8, 256), F32)
@@ -279,8 +284,10 @@
     sh, sl = split2(side)
 
     def along_z(mh, ml, ah, al, eh, el):
-        h0, h1, l0, l1 = mh[0:256], mh[256:384], ml[0:256], ml[256:384]
-        return dot(ah, h0) + dot(ah, l0) + dot(al, h0) + dot(eh, h1) + dot(eh, l1) + dot(el, h1)
+        high = jnp.concatenate([ah, eh], axis=1)
+        low = jnp.concatenate([al, el], axis=1)
+        twice = dot(jnp.concatenate([high, low], axis=0), mh)
+        return twice[0:128] + twice[128:256] + dot(high, ml)
 
     gz[...] = along_z(m1h[...], m1l[...], th, tl, sh, sl).reshape(4, 32, 256)
     lap[...] = along_z(m2h[...], m2l[...], th, tl, sh, sl).reshape(4, 32, 256)
@@ -294,7 +301,7 @@
         gy[p] = res[0:32]
         lap[p] += res[32:64]
 
-    for n in (4, 5, 6, 0, 1, 2, 3):
+    for n in (0, 1, 2, 3):
         b = 2 * senders[n] + core
         arrived(buf.at[slot(b)], a_send.at[n], a_recv.at[n], {"blk": b})
         pass_on(buf.at[slot(b)], senders[n])
@@ -361,17 +368,17 @@
     def plane_of(line):
         return buf[pl.ds(line, 24, stride=SLAB), :]
 
-    def refine_wide(value, target):
-        vt[...] = value
-        target[pl.ds(6, 18, stride=2), :] = 0.75 * vt[1:19] + 0.25 * vt[0:18]
-        target[pl.ds(7, 18, stride=2), :] = 0.75 * vt[1:19] + 0.25 * vt[2:20]
-
-    def refine_own(value, target):
-        vt[...] = value
-        target[pl.ds(0, 16, stride=2), :] = 0.75 * vt[2:18] + 0.25 * vt[1:17]
-        target[pl.ds(1, 16, stride=2), :] = 0.75 * vt[2:18] + 0.25 * vt[3:19]
-
-    refine_wide(plane_of(23), efine)
+    def refine_wide(value, target, n):
+        vt[n] = value
+        target[pl.ds(6, 18, stride=2), :] = 0.75 * vt[n, 1:19, :] + 0.25 * vt[n, 0:18, :]
+        target[pl.ds(7, 18, stride=2), :] = 0.75 * vt[n, 1:19, :] + 0.25 * vt[n, 2:20, :]
+
+    def refine_own(value, target, n):
+        vt[n] = value
+        target[pl.ds(0, 16, stride=2), :] = 0.75 * vt[n, 2:18, :] + 0.25 * vt[n, 1:17, :]
+        target[pl.ds(1, 16, stride=2), :] = 0.75 * vt[n, 2:18, :] + 0.25 * vt[n, 3:19, :]
+
+    refine_wide(plane_of(23), efine, 16)
     edge_wide = efine[...]
     edge_own = efine[8:40, :]
     planes0 = [plane_of(s) for s in range(9)]
@@ -379,14 +386,14 @@
         value = coef[t, 0:1, :] * planes0[0]
         for s in range(1, 9):
             value += coef[t, s : s + 1, :] * planes0[s]
-        refine_own(value, fine0.at[t])
+        refine_own(value, fine0.at[t], t)
     for c, target, refine in ((1, fine1, refine_wide), (2, fine2, refine_own)):
         planes = [plane_of(2 + 7 * c + s) for s in range(7)]
         for p in range(4):
             value = coef[p + 2, 1:2, :] * planes[0]
             for s in range(1, 7):
                 value += coef[p + 2, s + 1 : s + 2, :] * planes[s]
-            refine(value, target.at[p])
+            refine(value, target.at[p], 4 + 4 * c + p)
 
     lines = [(fine2[p], edge_own, 18 + p) for p in range(4)]
     lines += [(fine1[p], edge_wide, 10 + p) for p in range(4)]
@@ -398,7 +405,7 @@
     flow_side = dot(xh[0:128], rz[:, 256:384]) + dot(xl[0:128], rz[:, 256:384])
 
     fh, fl = split2(flow[0:128] * theta[...].reshape(128, 256))
-    eh, el = split2(flow_side * zrecv[...].T)
+    eh, el = split2(flow_side * side)
     total = flow[0:128] * gz[...].reshape(128, 256) + along_z(m1h[...], m1l[...], fh, fl, eh, el)
     out_ref[...] = 0.2 * lap[...] - 0.5 * total.reshape(4, 32, 256)
     for p in range(4):
@@ -459,7 +466,7 @@
             vm(2, 8, 256), vm(2, 8, 256), vm(2, 8, 128), vm(128, 128), vm(2, 8, 128), vm(2, 8, 128),
             vm(8 * SLAB, 128), vm(24 * SLAB, 128), vm(8, 16, 128), vm(24, 128), vm(256, 384, kind=BF16),
             vm(384, 256, kind=BF16), vm(384, 256, kind=BF16), vm(384, 256, kind=BF16), vm(384, 256, kind=BF16),
-            vm(64, 256, kind=BF16), vm(4, 48, 256), vm(24, 128),
+            vm(64, 256, kind=BF16), vm(4, 48, 256), vm(17, 24, 128),
             vm(8, 32, 128), vm(4, 48, 128), vm(4, 32, 128), vm(48, 128),
             vm(4, 32, 256), vm(4, 32, 256), vm(4, 32, 256), vm(4, 32, 256),
             sem(6), sem(2), sem(2), sem(2), sem(2), sem(2), sem(2), sem(2), sem(2), sem(2), sem(2),

time: 33.9 us -> 33.9 us (level)
  no operation moved by 1% of the time
where the time goes in v4:
time: 33.9 us; the launch traced here: 33.7 us
  Pallas kernels  32.3 us (95%)
  other arithmetic  0.73 us (2%)
  between operations  0.67 us (2%)
    pallas_call x1, Pallas kernels, local(): pl.pallas_call(kernel, out_shape=pltpu.VMEM((4, 32, 256), F32), in_specs=...  32.3 us
    add x1, other arithmetic, local(): theta_new = theta + 15.0 / 16.0 * section_new  0.73 us

profile of v4, /device:TPU:1, one launch (start us, length us, event | category | flops | bytes accessed | tf_op | source)
XLA Modules:
  0.0 33.7 jit_solution(70173531111011312)
XLA Ops:
  0.6 0.0 copy-start
  0.6 0.0 copy-start.1
  0.7 32.3 %shard_map.131 = f32[4,32,256]{2,1,0:T(8,128)S(1)} custom-call(s32[64]{0:T(128)} %lower.1, f32[4]{0:T(128)} %weight.1, f32[4]{0:T(128)} %metric.1, f32[4,4]{1,0:T(4,128)} %fx.1, f32[4,4]{1,0:T(4,128)} %sx.1, f32[4,32,256]{2,1,0:T(8,128)} %theta_in.1, f32[96,128]{1,0:T(8,128)} %bitcast.1, f32[32,32]{1,0:T(8,128)} %fy_in.1, f32[32,32]{1,0:T(8,128)} %sy_in.1, ...), custom_call_target="tpu_custom_call" | custom-call | tf_op jit(solution)/shard_map/pallas_call | solution.py:458
  33.0 0.0 copy-done
  33.0 0.0 copy-done.1
  33.0 0.7 %multiply_add_fusion = (f32[4,32,256]{2,1,0:T(8,128)}, f32[4,32,256]{2,1,0:T(8,128)}) fusion(f32[4,32,256]{2,1,0:T(8,128)S(1)} %copy-done, f32[4,32,256]{2,1,0:T(8,128)S(1)} %shard_map.131, f32[4,32,256]{2,1,0:T(8,128)S(1)} %copy-done.1), kind=kLoop, calls=%fused_computation | loop fusion | flops 163840 | bytes 655360 | tf_op jit(solution)/shard_map/add | solution.py:483
Async XLA Ops:
  0.6 32.3 %copy-start = (f32[4,32,256]{2,1,0:T(8,128)S(1)}, f32[4,32,256]{2,1,0:T(8,128)}, u32[]{:S(2)}) copy-start(f32[4,32,256]{2,1,0:T(8,128)} %theta_in.1) | copy-start | bytes 393220
  0.6 32.3 %copy-start.1 = (f32[4,32,256]{2,1,0:T(8,128)S(1)}, f32[4,32,256]{2,1,0:T(8,128)}, u32[]{:S(2)}) copy-start(f32[4,32,256]{2,1,0:T(8,128)} %param.13) | copy-start | bytes 393220
